TPU v7x, 1024 devices: a whole 8x8x8 slice. The times are simulated.
1024 devices in a mesh: lat: 8 (over z), lon: 128 (over x, y, core).
Axes of the slice: x: 8, y: 8, z: 8, core: 2. Of those that a mesh axis runs over, the one named last changes fastest.
Arguments:
- ensemble: bfloat16 [64, 2097152], P(None, ('lat', 'lon')), may hold values from -6 to 6
- leaf_basis: bfloat16 [16, 2097152], P(None, ('lat', 'lon')), may hold values from -0.75 to 0.75
- near_blocks: bfloat16 [32768, 64, 320], P(('lat', 'lon')), may hold values from -0.3125 to 0.3125
- local_transfer: float32 [1024, 64, 16, 16], P(('lat', 'lon')), may hold values from -1.5 to 1.5
- local_coupling: float32 [1024, 64, 16, 16], P(('lat', 'lon')), may hold values from -1 to 1
- upper_transfer: float32 [8, 256, 16, 16], P('lat'), may hold values from -1.5 to 1.5
- upper_coupling: float32 [8, 256, 16, 16], P('lat'), may hold values from -1 to 1
- pair_source: int32 [8, 128, 64], P('lat', 'lon'), may hold values from 0 to 95
- pair_target: int32 [8, 128, 64], P('lat', 'lon'), may hold values from 0 to 31
- pair_coupling: float32 [8, 128, 64, 16, 16], P('lat', 'lon'), may hold values from -1.5 to 1.5
Outputs:
- product_field: float32 [64, 2097152], P(None, ('lat', 'lon'))
Inputs may be any that keep to these rules, and one draw needn't show every extreme that they name: `pair_source`: a pair's source names a leaf of the band below for values under 32, of the own band under 2 * 32, else of the band above.
All inputs are finite; a program needn't handle non-finite values.
Results may differ from a plain program's by a relative error of at most 0.0006.
Values may be sent and summed in bfloat16 or wider, within the bound.
A program may use at most 32 MiB of HBM per device.

v0:
```python
import jax
import jax.numpy as jnp
from jax import lax
from jax.sharding import PartitionSpec as P


def extended_2(cells, sides, width):
    for axis, dim in sides:
        count = lax.axis_size(axis)
        ends = count - 1
        head = lax.slice_in_dim(cells, 0, width, axis=dim)
        tail = lax.slice_in_dim(cells, cells.shape[dim] - width, cells.shape[dim], axis=dim)
        cells = jnp.concatenate(
            [
                lax.ppermute(tail, axis, [(i, (i + 1) % count) for i in range(ends)]),
                cells,
                lax.ppermute(head, axis, [((i + 1) % count, i) for i in range(ends)]),
            ],
            axis=dim,
        )
    return cells


def from_partner(x, axis, apart):
    return lax.ppermute(x, axis, [(i, i ^ 1 << apart) for i in range(lax.axis_size(axis))])


def product(pattern, left_term, right_term):
    return jnp.einsum(pattern, left_term, right_term, precision=lax.Precision.HIGHEST)


def swapped_pairs(values):
    shaped = values.reshape((values.shape[0] // 2, 2) + values.shape[1:])
    return shaped[:, ::-1].reshape(values.shape)


def shards(
    ensemble,
    leaf_basis,
    near_blocks,
    local_transfer,
    local_coupling,
    upper_transfer,
    upper_coupling,
    pair_source,
    pair_target,
    pair_coupling,
):
    vector_count, point_count = ensemble.shape
    leaf_count, leaf_points, window_cols = near_blocks.shape
    rank_count = leaf_basis.shape[0]
    reach_leaves = window_cols // leaf_points // 2
    padded = extended_2(ensemble, ((("lat", "lon"), 1),), reach_leaves * leaf_points)
    padded_rows = jnp.transpose(
        padded.reshape(vector_count, leaf_count + 2 * reach_leaves, leaf_points), (1, 2, 0)
    )
    windows = jnp.concatenate(
        [padded_rows[offset : offset + leaf_count] for offset in range(2 * reach_leaves + 1)],
        axis=1,
    )
    near_rows = jnp.einsum("gik,gkr->gir", near_blocks, windows, preferred_element_type=jnp.float32)
    own_rows = padded_rows[reach_leaves : reach_leaves + leaf_count]
    basis_rows = jnp.transpose(leaf_basis.reshape(rank_count, leaf_count, leaf_points), (1, 0, 2))
    leaf_sums = jnp.einsum("gki,gir->gkr", basis_rows, own_rows, preferred_element_type=jnp.float32)
    extended = extended_2(leaf_sums, (("lat", 0),), leaf_count)
    edges_local = local_transfer[0]
    links_local = local_coupling[0]
    climbed = []
    current = leaf_sums
    level_width = leaf_count
    while level_width > 1:
        climbed.append(current)
        pushed = product("nab,nar->nbr", edges_local[level_width : 2 * level_width], current)
        current = pushed[0::2] + pushed[1::2]
        level_width = level_width // 2
    device_sum = current[0]
    lon_count = lax.axis_size("lon")
    tier_count = lon_count.bit_length() - 1
    heap_edges = upper_transfer[0]
    heap_links = upper_coupling[0]
    leaf_node = lon_count + lax.axis_index("lon")
    siblings = []
    own_sum = device_sum
    for tier_index in range(tier_count):
        other_sum = from_partner(own_sum, "lon", tier_index)
        siblings.append(other_sum)
        node_here = leaf_node // 2**tier_index
        own_edge = lax.dynamic_index_in_dim(heap_edges, node_here, 0, keepdims=False)
        other_edge = lax.dynamic_index_in_dim(
            heap_edges, node_here + 1 - 2 * (node_here % 2), 0, keepdims=False
        )
        own_sum = product("ab,ar->br", own_edge, own_sum) + product(
            "ab,ar->br", other_edge, other_sum
        )
    downward = jnp.zeros((rank_count, vector_count), jnp.float32)
    for tier_index in reversed(range(tier_count)):
        node_here = leaf_node // 2**tier_index
        edge_here = lax.dynamic_index_in_dim(heap_edges, node_here, 0, keepdims=False)
        link_here = lax.dynamic_index_in_dim(heap_links, node_here, 0, keepdims=False)
        downward = product("ab,br->ar", edge_here, downward) + product(
            "ab,br->ar", link_here, siblings[tier_index]
        )
    level_down = downward[None]
    level_width = 2
    for below in reversed(climbed):
        parents = jnp.repeat(level_down, 2, axis=0)
        level_down = product(
            "nab,nbr->nar", edges_local[level_width : 2 * level_width], parents
        ) + product(
            "nab,nbr->nar", links_local[level_width : 2 * level_width], swapped_pairs(below)
        )
        level_width = level_width * 2
    picked = jnp.take(extended, pair_source[0, 0], axis=0)
    coupled = product("pab,pbr->par", pair_coupling[0, 0], picked)
    targets = (
        pair_target[0, 0][:, None] == jnp.arange(leaf_count, dtype=jnp.int32)[None, :]
    ).astype(jnp.float32)
    leaf_down = level_down + product("pg,par->gar", targets, coupled)
    far_rows = product("gki,gkr->gir", basis_rows.astype(jnp.float32), leaf_down)
    total_rows = near_rows + far_rows
    return jnp.transpose(total_rows, (2, 0, 1)).reshape(vector_count, point_count)


def solution(mesh):
    return jax.shard_map(
        shards,
        mesh=mesh,
        in_specs=(
            P(None, ("lat", "lon")),
            P(None, ("lat", "lon")),
            P(("lat", "lon"), None, None),
            P(("lat", "lon"), None, None, None),
            P(("lat", "lon"), None, None, None),
            P("lat", None, None, None),
            P("lat", None, None, None),
            P("lat", "lon", None),
            P("lat", "lon", None),
            P("lat", "lon", None, None, None),
        ),
        out_specs=P(None, ("lat", "lon")),
        check_vma=False,
    )
```

profile of v0, /device:TPU:8, one launch (start us, length us, event | category | flops | bytes accessed | tf_op | source)
XLA Modules:
  0.0 151.9 jit_solution(2958376010895364402)
XLA Ops:
  1.5 1.9 %collective-permute-start = (bf16[64,128]{1,0:T(8,128)(2,1)}, bf16[64,128]{1,0:T(8,128)(2,1)}, u32[]{:S(2)}, u32[]{:S(2)}) collective-permute-start(bf16[64,128]{1,0:T(8,128)(2,1)} %get-tuple-element.30), channel_id=1, source_target_pairs={{0,1},{1,2},{2,3},{3,4},{4,5},{5,6},{6,7},{7,8},{8,9},{9,10},{10,1... | collective-permute-start | bytes 49160 | tf_op jit(solution)/shard_map/ppermute | solution.py:15
  3.4 7.0 %collective-permute-start.1 = (bf16[64,128]{1,0:T(8,128)(2,1)}, bf16[64,128]{1,0:T(8,128)(2,1)}, u32[]{:S(2)}, u32[]{:S(2)}) collective-permute-start(bf16[64,128]{1,0:T(8,128)(2,1)} %get-tuple-element.31), channel_id=1, source_target_pairs={{1,0},{2,1},{3,2},{4,3},{5,4},{6,5},{7,6},{8,7},{9,8},{10,9},{11,1... | collective-permute-start | bytes 49160 | tf_op jit(solution)/shard_map/ppermute | solution.py:17
  12.4 3.2 %constant_dynamic-slice_fusion = (f32[1,1,16,16]{1,3,2,0:T(8,128)S(1)}, f32[1,1,16,16]{1,3,2,0:T(8,128)S(1)}, f32[1,1,16,16]{1,3,2,0:T(8,128)S(1)}, f32[1,1,16,1...) fusion(f32[1,256,16,16]{1,3,2,0:T(8,128)} %param.16, ...), kind=kLoop, calls=%fused_computation.116 | loop fusion | bytes 41012 | tf_op jit(solution)/shard_map/jit(dynamic_index_in_dim)/dynamic_slice | solution.py:99
  27.8 1.7 %copy.123 = f32[1,2,16,16]{2,3,1,0:T(8,128)} copy(f32[1,2,16,16]{1,3,2,0:T(8,128)} %slice.142) | data formatting | bytes 4096
  29.4 1.7 %copy.124 = f32[1,1,16,16]{3,2,1,0:T(8,128)} copy(f32[1,1,16,16]{1,3,2,0:T(8,128)} %get-tuple-element.39) | data formatting | bytes 2048
  32.2 1.7 %copy.125 = f32[1,1,16,16]{3,2,1,0:T(8,128)} copy(f32[1,1,16,16]{1,3,2,0:T(8,128)} %get-tuple-element.40) | data formatting | bytes 2048
  33.8 1.7 %copy.113 = f32[1,1,16,16]{3,2,1,0:T(8,128)} copy(f32[1,1,16,16]{1,3,2,0:T(8,128)} %get-tuple-element.34) | data formatting | bytes 2048
  35.5 1.7 %copy.126 = f32[1,1,16,16]{3,2,1,0:T(8,128)} copy(f32[1,1,16,16]{1,3,2,0:T(8,128)} %get-tuple-element.41) | data formatting | bytes 2048
  37.2 1.7 %copy.114 = f32[1,1,16,16]{3,2,1,0:T(8,128)} copy(f32[1,1,16,16]{1,3,2,0:T(8,128)} %get-tuple-element.35) | data formatting | bytes 2048
  38.8 1.7 %copy.127 = f32[1,1,16,16]{3,2,1,0:T(8,128)} copy(f32[1,1,16,16]{1,3,2,0:T(8,128)} %get-tuple-element.42) | data formatting | bytes 2048
  40.5 1.7 %copy.115 = f32[1,1,16,16]{3,2,1,0:T(8,128)} copy(f32[1,1,16,16]{1,3,2,0:T(8,128)} %get-tuple-element.36) | data formatting | bytes 2048
  49.7 1.7 %copy.136 = f32[1,2,16,16]{3,2,1,0:T(8,128)} copy(f32[1,2,16,16]{1,3,2,0:T(8,128)} %slice.146) | data formatting | bytes 4096
  51.4 1.7 %copy.137 = f32[1,4,16,16]{3,2,1,0:T(8,128)} copy(f32[1,4,16,16]{1,3,2,0:T(8,128)} %slice.148) | data formatting | bytes 8192
  53.1 1.6 %copy.138 = f32[1,8,16,16]{3,2,1,0:T(8,128)} copy(f32[1,8,16,16]{1,3,2,0:T(8,128)} %slice.150) | data formatting | bytes 16384
  60.6 6.5 %collective-permute-start.9 = (f32[32,16,64]{2,1,0:T(8,128)S(1)}, f32[32,16,64]{2,1,0:T(8,128)}, u32[]{:S(2)}, u32[]{:S(2)}) collective-permute-start(f32[32,16,64]{2,1,0:T(8,128)S(1)} %bitcast.220), channel_id=1, source_target_pairs={{0,128},{128,256},{256,384},{384,512},{512,640},{640,768},{768,896... | collective-permute-start | bytes 393224 | tf_op jit(solution)/shard_map/ppermute | solution.py:15
  68.4 1.9 %collective-permute-start.2 = (f32[16,64]{1,0:T(8,128)S(1)}, f32[16,64]{1,0:T(8,128)S(1)}, u32[]{:S(2)}, u32[]{:S(2)}) collective-permute-start(f32[16,64]{1,0:T(8,128)S(1)} %fusion.40), channel_id=1, source_target_pairs={{0,1},{1,0},{2,3},{3,2},{4,5},{5,4},{6,7},{7,6},{8,9},{9,8},{10,11... | collective-permute-start | bytes 12296 | tf_op jit(solution)/shard_map/ppermute | solution.py:25
  71.7 1.9 %collective-permute-start.3 = (f32[16,64]{1,0:T(8,128)S(1)}, f32[16,64]{1,0:T(8,128)S(1)}, u32[]{:S(2)}, u32[]{:S(2)}) collective-permute-start(f32[16,64]{1,0:T(8,128)S(1)} %convolution_add_fusion.18), channel_id=1, source_target_pairs={{0,2},{1,3},{2,0},{3,1},{4,6},{5,7},{6,4},{7,5},{8,10},{9,11},{10,... | collective-permute-start | bytes 12296 | tf_op jit(solution)/shard_map/ppermute | solution.py:25
  73.8 3.4 %collective-permute-done.3 = f32[16,64]{1,0:T(8,128)S(1)} collective-permute-done((f32[16,64]{1,0:T(8,128)S(1)}, f32[16,64]{1,0:T(8,128)S(1)}, u32[]{:S(2)}, u32[]{:S(2)}) %collective-permute-start.3) | collective-permute-done | bytes 4128 | tf_op jit(solution)/shard_map/ppermute | solution.py:25
  77.4 1.9 %collective-permute-start.4 = (f32[16,64]{1,0:T(8,128)S(1)}, f32[16,64]{1,0:T(8,128)S(1)}, u32[]{:S(2)}, u32[]{:S(2)}) collective-permute-start(f32[16,64]{1,0:T(8,128)S(1)} %convolution_add_fusion.17), channel_id=1, source_target_pairs={{0,4},{1,5},{2,6},{3,7},{4,0},{5,1},{6,2},{7,3},{8,12},{9,13},{10,... | collective-permute-start | bytes 12296 | tf_op jit(solution)/shard_map/ppermute | solution.py:25
  79.5 4.3 %collective-permute-done.4 = f32[16,64]{1,0:T(8,128)S(1)} collective-permute-done((f32[16,64]{1,0:T(8,128)S(1)}, f32[16,64]{1,0:T(8,128)S(1)}, u32[]{:S(2)}, u32[]{:S(2)}) %collective-permute-start.4) | collective-permute-done | bytes 4128 | tf_op jit(solution)/shard_map/ppermute | solution.py:25
  84.0 6.1 %collective-permute-start.5 = (f32[16,64]{1,0:T(8,128)S(1)}, f32[16,64]{1,0:T(8,128)S(1)}, u32[]{:S(2)}, u32[]{:S(2)}) collective-permute-start(f32[16,64]{1,0:T(8,128)S(1)} %convolution_add_fusion.16), channel_id=1, source_target_pairs={{0,8},{1,9},{2,10},{3,11},{4,12},{5,13},{6,14},{7,15},{8,0},{9,1},... | collective-permute-start | bytes 12296 | tf_op jit(solution)/shard_map/ppermute | solution.py:25
  90.3 3.2 %collective-permute-done.5 = f32[16,64]{1,0:T(8,128)S(1)} collective-permute-done((f32[16,64]{1,0:T(8,128)S(1)}, f32[16,64]{1,0:T(8,128)S(1)}, u32[]{:S(2)}, u32[]{:S(2)}) %collective-permute-start.5) | collective-permute-done | bytes 4128 | tf_op jit(solution)/shard_map/ppermute | solution.py:25
  93.7 2.0 %collective-permute-start.6 = (f32[16,64]{1,0:T(8,128)S(1)}, f32[16,64]{1,0:T(8,128)S(1)}, u32[]{:S(2)}, u32[]{:S(2)}) collective-permute-start(f32[16,64]{1,0:T(8,128)S(1)} %convolution_add_fusion.15), channel_id=1, source_target_pairs={{0,16},{1,17},{2,18},{3,19},{4,20},{5,21},{6,22},{7,23},{8,24},{9,... | collective-permute-start | bytes 12296 | tf_op jit(solution)/shard_map/ppermute | solution.py:25
  95.9 3.3 %collective-permute-done.6 = f32[16,64]{1,0:T(8,128)S(1)} collective-permute-done((f32[16,64]{1,0:T(8,128)S(1)}, f32[16,64]{1,0:T(8,128)S(1)}, u32[]{:S(2)}, u32[]{:S(2)}) %collective-permute-start.6) | collective-permute-done | bytes 4128 | tf_op jit(solution)/shard_map/ppermute | solution.py:25
  99.4 2.0 %collective-permute-start.7 = (f32[16,64]{1,0:T(8,128)S(1)}, f32[16,64]{1,0:T(8,128)S(1)}, u32[]{:S(2)}, u32[]{:S(2)}) collective-permute-start(f32[16,64]{1,0:T(8,128)S(1)} %convolution_add_fusion.14), channel_id=1, source_target_pairs={{0,32},{1,33},{2,34},{3,35},{4,36},{5,37},{6,38},{7,39},{8,40},{9,... | collective-permute-start | bytes 12296 | tf_op jit(solution)/shard_map/ppermute | solution.py:25
  101.7 4.2 %collective-permute-done.7 = f32[16,64]{1,0:T(8,128)S(1)} collective-permute-done((f32[16,64]{1,0:T(8,128)S(1)}, f32[16,64]{1,0:T(8,128)S(1)}, u32[]{:S(2)}, u32[]{:S(2)}) %collective-permute-start.7) | collective-permute-done | bytes 4128 | tf_op jit(solution)/shard_map/ppermute | solution.py:25
  106.7 8.4 %collective-permute-start.8 = (f32[16,64]{1,0:T(8,128)}, f32[16,64]{1,0:T(8,128)}, u32[]{:S(2)}, u32[]{:S(2)}) collective-permute-start(f32[16,64]{1,0:T(8,128)} %convolution_add_fusion.13), channel_id=1, source_target_pairs={{0,64},{1,65},{2,66},{3,67},{4,68},{5,69},{6,70},{7,71},{8,72},{9,... | collective-permute-start | bytes 12296 | tf_op jit(solution)/shard_map/ppermute | solution.py:25
  115.1 1.6 %fusion.86 = (bf16[32,64,64]{1,2,0:T(8,128)(2,1)}, bf16[32,64,64]{1,2,0:T(8,128)(2,1)}, bf16[32,64,64]{1,2,0:T(8,128)(2,1)}, bf16[32,64,64]{1,2,0:T(8,128)(2,1)}, bf16[32,64,64]{1,2,0:T(8,128)(2,1)}) fusion(bf16[36,64,64]{1,2,0:T(8,128)(2,1)S(1)} %bitcast.218), kind=kLoop, calls=%fused_computation.144 | loop fusion | bytes 2621440 | tf_op jit(solution)/shard_map/slice | solution.py:58
  120.0 3.0 %concatenate.10 = bf16[32,320,64]{1,2,0:T(8,128)(2,1)S(1)} concatenate(bf16[32,64,64]{1,2,0:T(8,128)(2,1)} %get-tuple-element.9, bf16[32,64,64]{1,2,0:T(8,128)(2,1)} %get-tuple-element.8, bf16[32,64,64]{1,2,0:T(8,128)(2,1)} %get-tuple-element.7, bf16[32,64,64]{1,2,0:T(8,128)(2,1)} %get-tuple-element.6, bf16[32,64,64]{1,2,0:T(8,128)(2,1)} %get-tuple-element.5), dimensions={1} | concatenate | bytes 2621440 | tf_op jit(solution)/shard_map/concatenate | solution.py:57
  140.8 2.0 %pad_maximum_fusion = f32[96,16,64]{2,1,0:T(8,128)} fusion(f32[32,16,64]{2,1,0:T(8,128)} %collective-permute-done.10, f32[32,16,64]{2,1,0:T(8,128)S(1)} %bitcast.222, f32[32,16,64]{2,1,0:T(8,128)} %collective-permute-done.9), kind=kLoop, calls=%fused_computation.33 | loop fusion | flops 196608 | bytes 786432 | tf_op jit(solution)/shard_map/concatenate | solution.py:13
  142.7 2.7 %gather_fusion = f32[64,16,64]{2,1,0:T(8,128)} fusion(f32[96,16,64]{2,1,0:T(8,128)} %pad_maximum_fusion, s32[1024]{0:T(1024)} %pad_clamp_fusion), kind=kCustom, calls=%fused_computation | custom fusion | bytes 524544 | tf_op jit(solution)/shard_map/jit(_take)/gather | solution.py:113
  145.4 2.0 %convolution_bitcast_fusion = f32[64,16,64]{2,1,0:T(8,128)S(1)} fusion(f32[64,16,16]{2,1,0:T(8,128)} %copy.101, f32[64,16,64]{2,1,0:T(8,128)} %gather_fusion, pred[64]{0:T(512)(128)(4,1)S(1)} %copy-done.39), kind=kOutput, calls=%fused_computation.3 | convolution fusion | flops 12648448 | bytes 589888 | tf_op jit(solution)/shard_map/pab,pbr->par/dot_general | solution.py:29
  (188 shorter events, 60.3 us)
Async XLA Ops:
  0.0 149.4 %copy-start = (bf16[32,64,320]{2,1,0:T(8,128)(2,1)S(1)}, bf16[32,64,320]{2,1,0:T(8,128)(2,1)}, u32[]{:S(2)}) copy-start(bf16[32,64,320]{2,1,0:T(8,128)(2,1)} %param.12) | copy-start | bytes 3932164
  1.5 55.8 %collective-permute-start = (bf16[64,128]{1,0:T(8,128)(2,1)}, bf16[64,128]{1,0:T(8,128)(2,1)}, u32[]{:S(2)}, u32[]{:S(2)}) collective-permute-start(bf16[64,128]{1,0:T(8,128)(2,1)} %get-tuple-element.30), channel_id=1, source_target_pairs={{0,1},{1,2},{2,3},{3,4},{4,5},{5,6},{6,7},{7,8},{8,9},{9,10},{10,1... | collective-permute-start | bytes 49160 | tf_op jit(solution)/shard_map/ppermute | solution.py:15
  3.4 53.9 %collective-permute-start.1 = (bf16[64,128]{1,0:T(8,128)(2,1)}, bf16[64,128]{1,0:T(8,128)(2,1)}, u32[]{:S(2)}, u32[]{:S(2)}) collective-permute-start(bf16[64,128]{1,0:T(8,128)(2,1)} %get-tuple-element.31), channel_id=1, source_target_pairs={{1,0},{2,1},{3,2},{4,3},{5,4},{6,5},{7,6},{8,7},{9,8},{10,9},{11,1... | collective-permute-start | bytes 49160 | tf_op jit(solution)/shard_map/ppermute | solution.py:17
  22.4 19.7 %copy-start.13 = (f32[1,1,16,16]{1,3,2,0:T(8,128)S(1)}, f32[1,1,16,16]{1,3,2,0:T(8,128)}, u32[]{:S(2)}) copy-start(f32[1,1,16,16]{1,3,2,0:T(8,128)} %get-tuple-element.43) | copy-start | bytes 3076
  23.2 19.7 %copy-start.12 = (f32[1,1,16,16]{1,3,2,0:T(8,128)S(1)}, f32[1,1,16,16]{1,3,2,0:T(8,128)}, u32[]{:S(2)}) copy-start(f32[1,1,16,16]{1,3,2,0:T(8,128)} %get-tuple-element.37) | copy-start | bytes 3076
  24.3 34.4 %copy-start.6 = (bf16[16,32,64]{2,1,0:T(8,128)(2,1)}, bf16[16,32,64]{2,1,0:T(8,128)(2,1)S(1)}, u32[]{:S(2)}) copy-start(bf16[16,32,64]{2,1,0:T(8,128)(2,1)S(1)} %reshape.140) | copy-start | bytes 196612
  24.5 42.7 %copy-start.4 = (f32[1,32,16,16]{2,3,1,0:T(8,128)}, f32[1,32,16,16]{2,3,1,0:T(8,128)S(1)}, u32[]{:S(2)}) copy-start(f32[1,32,16,16]{2,3,1,0:T(8,128)S(1)} %copy.119) | copy-start | bytes 98308
  26.6 41.2 %copy-start.11 = (f32[1,8,16,16]{2,3,1,0:T(8,128)}, f32[1,8,16,16]{2,3,1,0:T(8,128)S(1)}, u32[]{:S(2)}) copy-start(f32[1,8,16,16]{2,3,1,0:T(8,128)S(1)} %copy.121) | copy-start | bytes 24580
  27.8 40.3 %copy-start.19 = (f32[1,4,16,16]{2,3,1,0:T(8,128)}, f32[1,4,16,16]{2,3,1,0:T(8,128)S(1)}, u32[]{:S(2)}) copy-start(f32[1,4,16,16]{2,3,1,0:T(8,128)S(1)} %copy.122) | copy-start | bytes 12292
  59.1 18.1 %copy-start.31 = (f32[1,1,16,16]{3,2,1,0:T(8,128)S(1)}, f32[1,1,16,16]{3,2,1,0:T(8,128)}, u32[]{:S(2)}) copy-start(f32[1,1,16,16]{3,2,1,0:T(8,128)} %copy.125) | copy-start | bytes 3076
  59.1 20.2 %copy-start.21 = (f32[1,1,16,16]{3,2,1,0:T(8,128)S(1)}, f32[1,1,16,16]{3,2,1,0:T(8,128)}, u32[]{:S(2)}) copy-start(f32[1,1,16,16]{3,2,1,0:T(8,128)} %copy.113) | copy-start | bytes 3076
  59.1 24.7 %copy-start.30 = (f32[1,1,16,16]{3,2,1,0:T(8,128)S(1)}, f32[1,1,16,16]{3,2,1,0:T(8,128)}, u32[]{:S(2)}) copy-start(f32[1,1,16,16]{3,2,1,0:T(8,128)} %copy.126) | copy-start | bytes 3076
  59.1 31.0 %copy-start.22 = (f32[1,1,16,16]{3,2,1,0:T(8,128)S(1)}, f32[1,1,16,16]{3,2,1,0:T(8,128)}, u32[]{:S(2)}) copy-start(f32[1,1,16,16]{3,2,1,0:T(8,128)} %copy.114) | copy-start | bytes 3076
  59.1 34.4 %copy-start.29 = (f32[1,1,16,16]{3,2,1,0:T(8,128)S(1)}, f32[1,1,16,16]{3,2,1,0:T(8,128)}, u32[]{:S(2)}) copy-start(f32[1,1,16,16]{3,2,1,0:T(8,128)} %copy.127) | copy-start | bytes 3076
  59.2 36.6 %copy-start.23 = (f32[1,1,16,16]{3,2,1,0:T(8,128)S(1)}, f32[1,1,16,16]{3,2,1,0:T(8,128)}, u32[]{:S(2)}) copy-start(f32[1,1,16,16]{3,2,1,0:T(8,128)} %copy.115) | copy-start | bytes 3076
  59.2 40.1 %copy-start.28 = (f32[1,1,16,16]{3,2,1,0:T(8,128)S(1)}, f32[1,1,16,16]{3,2,1,0:T(8,128)}, u32[]{:S(2)}) copy-start(f32[1,1,16,16]{3,2,1,0:T(8,128)} %copy.128) | copy-start | bytes 3076
  59.2 42.3 %copy-start.24 = (f32[1,1,16,16]{3,2,1,0:T(8,128)S(1)}, f32[1,1,16,16]{3,2,1,0:T(8,128)}, u32[]{:S(2)}) copy-start(f32[1,1,16,16]{3,2,1,0:T(8,128)} %copy.116) | copy-start | bytes 3076
  59.2 46.7 %copy-start.27 = (f32[1,1,16,16]{3,2,1,0:T(8,128)S(1)}, f32[1,1,16,16]{3,2,1,0:T(8,128)}, u32[]{:S(2)}) copy-start(f32[1,1,16,16]{3,2,1,0:T(8,128)} %copy.129) | copy-start | bytes 3076
  59.2 81.6 %collective-permute-start.10 = (f32[32,16,64]{2,1,0:T(8,128)S(1)}, f32[32,16,64]{2,1,0:T(8,128)}, u32[]{:S(2)}, u32[]{:S(2)}) collective-permute-start(f32[32,16,64]{2,1,0:T(8,128)S(1)} %bitcast.219), channel_id=1, source_target_pairs={{128,0},{256,128},{384,256},{512,384},{640,512},{768,640},{896,768... | collective-permute-start | bytes 393224 | tf_op jit(solution)/shard_map/ppermute | solution.py:17
  60.6 80.1 %collective-permute-start.9 = (f32[32,16,64]{2,1,0:T(8,128)S(1)}, f32[32,16,64]{2,1,0:T(8,128)}, u32[]{:S(2)}, u32[]{:S(2)}) collective-permute-start(f32[32,16,64]{2,1,0:T(8,128)S(1)} %bitcast.220), channel_id=1, source_target_pairs={{0,128},{128,256},{256,384},{384,512},{512,640},{640,768},{768,896... | collective-permute-start | bytes 393224 | tf_op jit(solution)/shard_map/ppermute | solution.py:15
  68.4 3.1 %collective-permute-start.2 = (f32[16,64]{1,0:T(8,128)S(1)}, f32[16,64]{1,0:T(8,128)S(1)}, u32[]{:S(2)}, u32[]{:S(2)}) collective-permute-start(f32[16,64]{1,0:T(8,128)S(1)} %fusion.40), channel_id=1, source_target_pairs={{0,1},{1,0},{2,3},{3,2},{4,5},{5,4},{6,7},{7,6},{8,9},{9,8},{10,11... | collective-permute-start | bytes 12296 | tf_op jit(solution)/shard_map/ppermute | solution.py:25
  71.5 45.2 %copy-start.33 = (f32[16,64]{1,0:T(8,128)}, f32[16,64]{1,0:T(8,128)S(1)}, u32[]{:S(2)}) copy-start(f32[16,64]{1,0:T(8,128)S(1)} %collective-permute-done.2) | copy-start | bytes 12292
  71.7 5.5 %collective-permute-start.3 = (f32[16,64]{1,0:T(8,128)S(1)}, f32[16,64]{1,0:T(8,128)S(1)}, u32[]{:S(2)}, u32[]{:S(2)}) collective-permute-start(f32[16,64]{1,0:T(8,128)S(1)} %convolution_add_fusion.18), channel_id=1, source_target_pairs={{0,2},{1,3},{2,0},{3,1},{4,6},{5,7},{6,4},{7,5},{8,10},{9,11},{10,... | collective-permute-start | bytes 12296 | tf_op jit(solution)/shard_map/ppermute | solution.py:25
  77.2 39.5 %copy-start.34 = (f32[16,64]{1,0:T(8,128)}, f32[16,64]{1,0:T(8,128)S(1)}, u32[]{:S(2)}) copy-start(f32[16,64]{1,0:T(8,128)S(1)} %collective-permute-done.3) | copy-start | bytes 12292
  77.4 6.4 %collective-permute-start.4 = (f32[16,64]{1,0:T(8,128)S(1)}, f32[16,64]{1,0:T(8,128)S(1)}, u32[]{:S(2)}, u32[]{:S(2)}) collective-permute-start(f32[16,64]{1,0:T(8,128)S(1)} %convolution_add_fusion.17), channel_id=1, source_target_pairs={{0,4},{1,5},{2,6},{3,7},{4,0},{5,1},{6,2},{7,3},{8,12},{9,13},{10,... | collective-permute-start | bytes 12296 | tf_op jit(solution)/shard_map/ppermute | solution.py:25
  83.9 32.9 %copy-start.35 = (f32[16,64]{1,0:T(8,128)}, f32[16,64]{1,0:T(8,128)S(1)}, u32[]{:S(2)}) copy-start(f32[16,64]{1,0:T(8,128)S(1)} %collective-permute-done.4) | copy-start | bytes 12292
  84.0 9.5 %collective-permute-start.5 = (f32[16,64]{1,0:T(8,128)S(1)}, f32[16,64]{1,0:T(8,128)S(1)}, u32[]{:S(2)}, u32[]{:S(2)}) collective-permute-start(f32[16,64]{1,0:T(8,128)S(1)} %convolution_add_fusion.16), channel_id=1, source_target_pairs={{0,8},{1,9},{2,10},{3,11},{4,12},{5,13},{6,14},{7,15},{8,0},{9,1},... | collective-permute-start | bytes 12296 | tf_op jit(solution)/shard_map/ppermute | solution.py:25
  93.5 23.2 %copy-start.36 = (f32[16,64]{1,0:T(8,128)}, f32[16,64]{1,0:T(8,128)S(1)}, u32[]{:S(2)}) copy-start(f32[16,64]{1,0:T(8,128)S(1)} %collective-permute-done.5) | copy-start | bytes 12292
  93.7 5.5 %collective-permute-start.6 = (f32[16,64]{1,0:T(8,128)S(1)}, f32[16,64]{1,0:T(8,128)S(1)}, u32[]{:S(2)}, u32[]{:S(2)}) collective-permute-start(f32[16,64]{1,0:T(8,128)S(1)} %convolution_add_fusion.15), channel_id=1, source_target_pairs={{0,16},{1,17},{2,18},{3,19},{4,20},{5,21},{6,22},{7,23},{8,24},{9,... | collective-permute-start | bytes 12296 | tf_op jit(solution)/shard_map/ppermute | solution.py:25
  99.2 17.5 %copy-start.37 = (f32[16,64]{1,0:T(8,128)}, f32[16,64]{1,0:T(8,128)S(1)}, u32[]{:S(2)}) copy-start(f32[16,64]{1,0:T(8,128)S(1)} %collective-permute-done.6) | copy-start | bytes 12292
  99.4 6.4 %collective-permute-start.7 = (f32[16,64]{1,0:T(8,128)S(1)}, f32[16,64]{1,0:T(8,128)S(1)}, u32[]{:S(2)}, u32[]{:S(2)}) collective-permute-start(f32[16,64]{1,0:T(8,128)S(1)} %convolution_add_fusion.14), channel_id=1, source_target_pairs={{0,32},{1,33},{2,34},{3,35},{4,36},{5,37},{6,38},{7,39},{8,40},{9,... | collective-permute-start | bytes 12296 | tf_op jit(solution)/shard_map/ppermute | solution.py:25
  106.7 16.4 %collective-permute-start.8 = (f32[16,64]{1,0:T(8,128)}, f32[16,64]{1,0:T(8,128)}, u32[]{:S(2)}, u32[]{:S(2)}) collective-permute-start(f32[16,64]{1,0:T(8,128)} %convolution_add_fusion.13), channel_id=1, source_target_pairs={{0,64},{1,65},{2,66},{3,67},{4,68},{5,69},{6,70},{7,71},{8,72},{9,... | collective-permute-start | bytes 12296 | tf_op jit(solution)/shard_map/ppermute | solution.py:25
  (20 other events, 184.4 us)
where the time goes:
time: 154 us; the launch traced here: 152 us
  local copies, waits for them, and re-layouts  58.2 us (38%)
  starting transfers between devices  41.2 us (27%)
  matrix products  27.2 us (18%)
  waiting for transfers between devices  19.4 us (13%)
  other arithmetic  5.21 us (3%)
    unnamed x112, local copies, waits for them, and re-layouts  32.4 us
    dot_general x44, matrix products, product(): jnp.einsum(pattern, left_term, right_term, precision=lax.Precision.HIGHEST)  26.2 us
    ppermute x7, starting transfers between devices, from_partner(): lax.ppermute(x, axis, [(i, i ^ 1 << apart) for i in range(lax.axis_size(a...  24.3 us
    ppermute x7, waiting for transfers between devices, from_partner(): lax.ppermute(x, axis, [(i, i ^ 1 << apart) for i in range(lax.axis_size(a...  19.3 us
    ppermute x2, starting transfers between devices, extended_2(): lax.ppermute(tail, axis, [(i, (i + 1) % count) for i in range(ends)])  8.44 us
    ppermute x2, starting transfers between devices, extended_2(): lax.ppermute(head, axis, [((i + 1) % count, i) for i in range(ends)])  8.39 us
    slice x5, local copies, waits for them, and re-layouts, shards(): links_local[level_width:2 * level_width]  3.76 us
    dynamic_slice x1, local copies, waits for them, and re-layouts, shards(): lax.dynamic_index_in_dim(heap_links, node_here, 0, keepdims=False)  3.16 us
  transfers between devices with their start and end apart: 11, of which 6 were waited for; matrix products, arithmetic and copies ran while one was open for 50% of the time, Pallas kernels for 0%

commit v1 on v0

v1 whole, which is shorter than its diff:
```python
import functools

import jax
import jax.numpy as jnp
from jax import lax
from jax.experimental import pallas as pl
from jax.experimental.pallas import tpu as pltpu
from jax.sharding import PartitionSpec as P

F32 = jnp.float32
BF16 = jnp.bfloat16
RANK = 16
LANES = 128
NODES = 8
MESH = pl.DeviceIdType.MESH


def iota(shape, axis):
    return lax.broadcasted_iota(jnp.int32, shape, axis)


def one_hot(mask):
    return jnp.where(mask, 1.0, 0.0).astype(BF16)


def nn(a, b):
    return lax.dot_general(a, b, (((1,), (0,)), ((), ())), preferred_element_type=F32)


def nt(a, b):
    return lax.dot_general(a, b, (((1,), (1,)), ((), ())), preferred_element_type=F32)


def split(x):
    high = x.astype(BF16)
    return high, (x - high.astype(F32)).astype(BF16)


def three(dot, a, b):
    return dot(a[0], b[0]) + (dot(a[0], b[1]) + dot(a[1], b[0]))


def picked_by(dot, a, b):
    return dot(a[0], b) + dot(a[1], b)


def picks(dot, a, b):
    return dot(a, b[0]) + dot(a, b[1])


def side_by_side(parts):
    return jnp.concatenate(parts, axis=1)


def rows_of(refs, first, count):
    return tuple(ref[pl.ds(first * LANES, count * LANES), :] for ref in refs)


def climb(leaves, count, edge):
    ups = {}
    if count < NODES:
        ups[0] = leaves[0]
    else:
        level = count // NODES
        for i, block in enumerate(leaves):
            ups[level + i] = block
        while level > 1:
            for i in range(level // 2, level):
                pair = side_by_side([ups[2 * i], ups[2 * i + 1]])
                ups[i] = three(nn, split(pair), edge(2 * i, 2))
            level //= 2
        ups[0] = three(nn, split(ups[1]), edge(1, 1))
    if count >= 4:
        ups[0] = ups[0] + three(nn, split(ups[0]), edge(0, 1))
    return ups


def descend(ups, count, edge, link):
    rows = ups[0].shape[0]
    top = three(nt, split(ups[0]), link(0, 1))
    if count >= 4:
        slot = iota((rows, LANES), 1) % NODES
        first = jnp.where((slot == 2) | (slot == 3), top, 0.0)
        top = top + three(nt, split(first), edge(0, 1))
    if count < NODES:
        return [top]
    level = [three(nt, split(ups[1]), link(1, 1)) + three(nt, split(top), edge(1, 1))]
    while len(level) < count // NODES:
        width = len(level)
        below = []
        for i, block in enumerate(level):
            node = width + i
            both = three(nt, split(block), edge(2 * node, 2))
            for side in range(2):
                child = 2 * node + side
                own = three(nt, split(ups[child]), link(child, 1))
                below.append(own + both[:, side * LANES : (side + 1) * LANES])
        level = below
    return level


def paths(count, edge):
    levels = []
    start = one_hot(iota((RANK, LANES), 1) == iota((RANK, LANES), 0) * NODES + 1)
    step = picks(nt, start, edge(0, 1))
    if count >= 4:
        step = three(nt, split(step), edge(0, 1))
    if count < NODES:
        return [[step]]
    levels.append([three(nt, split(step), edge(1, 1))])
    while len(levels[-1]) < count // NODES:
        width = len(levels[-1])
        below = []
        for i, block in enumerate(levels[-1]):
            both = three(nt, split(block), edge(2 * (width + i), 2))
            below += [both[:, :LANES], both[:, LANES:]]
        levels.append(below)
    return levels


def stacked(blocks):
    count = blocks
    members = min(count, NODES)
    offset = count if count < NODES else 0
    row = iota((members * RANK, LANES), 0)
    lane = iota((members * RANK, LANES), 1)
    return one_hot(lane == (row % RANK) * NODES + row // RANK + offset)


def operators(turned, masks, edge_refs, block, spread):
    (high, low), mask = turned, masks
    nodes = high.shape[0]
    for half in range(2):
        cut = slice(half * LANES, (half + 1) * LANES)
        both = jnp.concatenate([high[:, cut], low[:, cut]], axis=0)
        for pair in range(NODES // 2):
            wide = nn(both, spread[pair])
            parts = [
                [
                    jnp.where(mask, wide[k * nodes : (k + 1) * nodes, s * LANES : (s + 1) * LANES], 0.0)
                    for s in range(2)
                ]
                for k in range(2)
            ]
            for k in range(2):
                for j in range(nodes // NODES):
                    rows = slice(j * NODES, (j + 1) * NODES)
                    tile = jnp.concatenate([parts[k][0][rows], parts[k][1][rows]], axis=0)
                    start = (block + j) * LANES + (half * NODES + 2 * pair) * NODES
                    edge_refs[k][start : start + 2 * NODES, :] = tile.astype(BF16)


def kernel(
    sizes,
    ensemble,
    basis,
    near,
    local_edge,
    local_link,
    upper_edge,
    upper_link,
    source,
    target,
    pair_link,
    out_ref,
    x_ref,
    basis_ref,
    near_ref,
    le_ref,
    ll_ref,
    ue_ref,
    ul_ref,
    src_ref,
    tgt_ref,
    pl_ref,
    eh_ref,
    el_ref,
    vh_ref,
    vl_ref,
    basis_blocks,
    ext_ref,
    members_ref,
    groups_ref,
    final_ref,
    load_sem,
    send_sem,
    member_sem,
    group_sem,
    side_sem,
):
    n_lat, groups, members = sizes
    n_lon = groups * members
    vectors, points = ensemble.shape
    leaves = near.shape[0]
    leaf_points = near.shape[1]
    halo = near.shape[2] // 2 - leaf_points // 2
    lat, lon = lax.axis_index("lat"), lax.axis_index("lon")
    group, member = lon // members, lon % members
    flat = lat * n_lon + lon
    total = n_lat * n_lon

    def at(index):
        index = lax.rem(index, total)
        return (index // n_lon, lax.rem(index, n_lon))

    member_peers = [(lat, group * members + lax.rem(member + j, members)) for j in range(1, members)]
    group_peers = [(lat, lax.rem(group + j, groups) * members + member) for j in range(1, groups)]
    above = (lax.rem(lat + 1, n_lat), lon)
    below = (lax.rem(lat + n_lat - 1, n_lat), lon)
    after, before = at(flat + 1), at(flat + total - 1)

    own_points = x_ref.at[:, halo : halo + points]
    loads = [
        pltpu.make_async_copy(src, dst, load_sem.at[i])
        for i, (src, dst) in enumerate(
            [
                (local_edge, le_ref),
                (basis, basis_ref),
                (ensemble, own_points),
                (local_link, ll_ref),
                (upper_edge, ue_ref),
                (upper_link, ul_ref),
                (source, src_ref),
                (target, tgt_ref),
                (pair_link, pl_ref),
                (near, near_ref),
            ]
        )
    ]
    for load in loads:
        load.start()

    barrier = pltpu.get_barrier_semaphore()
    peers = member_peers + group_peers + [above, below, after, before]
    for peer in peers:
        pl.semaphore_signal(barrier, inc=1, device_id=peer, device_id_type=MESH)

    row, lane = iota((LANES, LANES), 0), iota((LANES, LANES), 1)
    offset = row - lane // NODES
    spread = []
    for pair in range(NODES // 2):
        spread.append(
            side_by_side([one_hot(offset == (2 * pair + s) * RANK) for s in range(2)])
        )

    def masks(count, slots):
        node_slot = slots(iota((count, LANES), 0))
        column = iota((count, LANES), 1) % NODES
        inner = node_slot >= 2
        edge = inner & (column == (node_slot // 2) % NODES)
        link = inner & (column == (node_slot + 1 - 2 * (node_slot % 2)) % NODES)
        return edge, link

    eye = one_hot(iota((2 * leaves, 2 * leaves), 0) == iota((2 * leaves, 2 * leaves), 1))
    local_masks = masks(2 * leaves, lambda r: r)

    def turned(ref, chosen):
        parts = split(ref[...])
        return tuple(nt(chosen, part).astype(BF16) for part in parts)

    edges, links = (eh_ref, el_ref), (vh_ref, vl_ref)
    local_blocks = 2 * leaves // NODES
    member_blocks = max(1, 2 * members // NODES)
    group_blocks = max(1, 2 * groups // NODES)

    def reader(refs, base):
        return lambda first, count: rows_of(refs, base + first, count)

    local_e, local_v = reader(edges, 0), reader(links, 0)
    member_e, member_v = reader(edges, local_blocks), reader(links, local_blocks)
    group_base = local_blocks + member_blocks
    group_e, group_v = reader(edges, group_base), reader(links, group_base)

    loads[0].wait()
    operators(turned(le_ref, eye), local_masks[0], edges, 0, spread)

    loads[1].wait()
    width = NODES * leaf_points
    leaf_blocks = leaves // NODES
    keep = iota((NODES, width), 0) == iota((NODES, width), 1) // leaf_points
    for j in range(leaf_blocks):
        part = basis_ref[:, j * width : (j + 1) * width].astype(F32)
        for k in range(0, RANK, 2):
            tiles = [
                jnp.where(keep, jnp.broadcast_to(part[k + s : k + s + 1], (NODES, width)), 0.0)
                for s in range(2)
            ]
            basis_blocks[j, k * NODES : (k + 2) * NODES, :] = jnp.concatenate(tiles, axis=0).astype(BF16)
    loads[2].wait()
    sums_across = []
    for j in range(leaf_blocks):
        x_part = x_ref[:, halo + j * width : halo + (j + 1) * width]
        sums_across.append(nt(x_part, basis_blocks[j]))
        by_rank = nt(basis_blocks[j], x_part)
        for k in range(RANK // 2):
            ext_ref[leaves + j * NODES : leaves + (j + 1) * NODES, k * LANES : (k + 1) * LANES] = side_by_side(
                [
                    by_rank[k * NODES : (k + 1) * NODES],
                    by_rank[(k + RANK // 2) * NODES : (k + RANK // 2 + 1) * NODES],
                ]
            )

    local_ups = climb(sums_across, leaves, local_e)
    local_paths = paths(leaves, local_e)
    device_sum = three(nt, split(local_paths[0][0]), split(local_ups[1]))
    empty = jnp.zeros((RANK, LANES - vectors), F32)
    own_member = members_ref.at[pl.ds(member * RANK, RANK)]
    own_member[...] = side_by_side([device_sum, empty])

    pl.semaphore_wait(barrier, len(peers))

    def send(src, dst, index, arrived, peer):
        copy = pltpu.make_async_remote_copy(
            src_ref=src,
            dst_ref=dst,
            send_sem=send_sem.at[index],
            recv_sem=arrived,
            device_id=peer,
            device_id_type=MESH,
        )
        copy.start()
        return copy

    member_copies = [
        send(own_member, own_member, j, member_sem.at[j], peer) for j, peer in enumerate(member_peers)
    ]
    used = len(member_peers)
    own_sums = ext_ref.at[leaves : 2 * leaves]
    side_copies = [
        send(x_ref.at[:, points : points + halo], x_ref.at[:, 0:halo], used, side_sem.at[0], after),
        send(
            x_ref.at[:, halo : 2 * halo],
            x_ref.at[:, halo + points : points + 2 * halo],
            used + 1,
            side_sem.at[1],
            before,
        ),
        send(own_sums, ext_ref.at[0:leaves], used + 2, side_sem.at[2], above),
        send(own_sums, ext_ref.at[2 * leaves : 3 * leaves], used + 3, side_sem.at[3], below),
    ]
    used += 4

    member_slots, group_slots = member_blocks * NODES, group_blocks * NODES
    upper_rows = member_slots + group_slots
    upper_nodes = upper_edge.shape[1]
    slot = iota((upper_rows, upper_nodes), 0)
    scale = jnp.where(slot >= 2, 2, 1)
    for power in range(2, members.bit_length()):
        scale = jnp.where(slot >= 2**power, 2**power, scale)
    wanted = jnp.where(slot < member_slots, slot + (groups + group - 1) * scale, slot - member_slots)
    chosen = one_hot(wanted == iota((upper_rows, upper_nodes), 1))
    upper_masks = masks(upper_rows, lambda r: jnp.where(r < member_slots, r, r - member_slots))
    loads[4].wait()
    operators(turned(ue_ref, chosen), upper_masks[0], edges, local_blocks, spread)

    member_order = stacked(members)
    member_paths = paths(members, member_e)[-1]
    to_group = [split(picked_by(nt, split(block), member_order)) for block in member_paths]

    loads[3].wait()
    operators(turned(ll_ref, eye), local_masks[1], links, 0, spread)
    loads[5].wait()
    operators(turned(ul_ref, chosen), upper_masks[1], links, local_blocks, spread)

    for copy in member_copies:
        copy.wait_recv()
    member_sums = members_ref[...]
    member_parts = split(member_sums)
    per_block = min(members, NODES) * RANK
    group_sum = None
    for i, block in enumerate(to_group):
        cut = slice(i * per_block, (i + 1) * per_block)
        term = three(nn, block, (member_parts[0][cut], member_parts[1][cut]))
        group_sum = term if group_sum is None else group_sum + term
    own_group = groups_ref.at[pl.ds(group * RANK, RANK)]
    own_group[...] = group_sum

    group_copies = [
        send(own_group, own_group, used + j, group_sem.at[j], peer) for j, peer in enumerate(group_peers)
    ]

    repeat = iota((LANES, LANES), 1)
    rank_lane = jnp.where(repeat < 3 * RANK, repeat % RANK, -1)
    own_slots = []
    for i in range(len(member_paths)):
        mine = member - i * NODES if members >= NODES else member + members
        own_slots.append(one_hot((row // NODES == rank_lane) & (row % NODES == mine)))
    own_path = None
    for block, pick in zip(member_paths, own_slots):
        term = picked_by(nn, split(block), pick)
        own_path = term if own_path is None else own_path + term
    group_slot = group if groups >= NODES else group + groups
    lift = one_hot(
        (iota((LANES, RANK), 0) // NODES == iota((LANES, RANK), 1))
        & (iota((LANES, RANK), 0) % NODES == group_slot)
    )
    lifted = split(picks(nn, lift, split(own_path)))
    group_ups = climb([stacked(groups).astype(F32)], groups, group_e)
    group_map = descend(group_ups, groups, group_e, group_v)[0]
    group_map = split(three(nn, split(group_map), lifted))

    member_across = []
    turned_sums = jnp.transpose(member_sums)[:vectors]
    for i in range(len(member_paths)):
        part = split(turned_sums[:, i * per_block : (i + 1) * per_block])
        member_across.append(picked_by(nn, part, member_order))
    member_ups = climb(member_across, members, member_e)
    down_here = None
    for block, pick in zip(descend(member_ups, members, member_e, member_v), own_slots):
        term = picked_by(nn, split(block), pick)
        down_here = term if down_here is None else down_here + term

    for j in range(leaf_blocks):
        folded = split(picked_by(nn, split(local_paths[-1][j]), basis_blocks[j]))
        cut = slice(j * width, (j + 1) * width)
        final_ref[0:RANK, cut] = folded[0]
        final_ref[RANK : 2 * RANK, cut] = folded[0]
        final_ref[2 * RANK : 3 * RANK, cut] = folded[1]

    local_down = descend(local_ups, leaves, local_e, local_v)

    loads[9].wait()
    side_copies[0].wait_recv()
    side_copies[1].wait_recv()

    @pl.when(flat == 0)
    def _():
        x_ref[:, 0:halo] = jnp.zeros((vectors, halo), BF16)

    @pl.when(flat == total - 1)
    def _():
        x_ref[:, halo + points :] = jnp.zeros((vectors, halo), BF16)

    blank = jnp.zeros((leaf_points, leaf_points), BF16)
    pair_points = 2 * leaf_points
    span = near.shape[2] + leaf_points
    for j in range(leaves // 2):
        first = side_by_side([near_ref[2 * j], blank])
        second = side_by_side([blank, near_ref[2 * j + 1]])
        weights = jnp.concatenate([first, second], axis=0)
        window = x_ref[:, j * pair_points : j * pair_points + span]
        out_ref[:, j * pair_points : (j + 1) * pair_points] = nt(window, weights)

    for load in loads[6:9]:
        load.wait()
    side_copies[2].wait_recv()
    side_copies[3].wait_recv()
    pairs = source.shape[1]
    spot = iota((3 * leaves, pairs), 0)
    inside = ((spot >= leaves) | (lat > 0)) & ((spot < 2 * leaves) | (lat < n_lat - 1))
    reads = jnp.where((spot == src_ref[...]) & inside, 1.0, 0.0)
    reads = jnp.transpose(reads).astype(BF16)
    found = [nn(reads, part) for part in split(ext_ref[...])]
    half = RANK // 2
    wide_target = side_by_side([tgt_ref[...], tgt_ref[...]])
    hits = jnp.where(iota((leaves, 2 * pairs), 0) == wide_target, 1.0, 0.0)
    link_rows = pl_ref[...].reshape(RANK, 2, half, pairs)
    link_rows = jnp.concatenate([link_rows[:, 0], link_rows[:, 1]], axis=2)
    link_high = link_rows.astype(BF16).astype(F32)
    link_parts = (link_high, link_rows - link_high)
    rights = [[], []]
    for k in range(half):
        for s in range(2):
            tile = found[s][:, k * LANES : (k + 1) * LANES]
            rights[s].append(jnp.concatenate([tile[:, :vectors], tile[:, vectors:]], axis=0))
    rights = [jnp.concatenate(r, axis=0).astype(BF16) for r in rights]
    for j in range(leaf_blocks):
        hit = hits[j * NODES : (j + 1) * NODES]
        lefts = []
        for part in link_parts:
            columns = []
            for k in range(half):
                columns.append(
                    jnp.concatenate([hit * part[a, k : k + 1] for a in range(RANK)], axis=0).astype(BF16)
                )
            lefts.append(side_by_side(columns))
        added = three(nn, lefts, rights)
        down = local_down[j] + jnp.transpose(added)
        cut = slice(j * width, (j + 1) * width)
        out_ref[:, cut] = out_ref[:, cut] + picked_by(nn, split(down), basis_blocks[j])

    for copy in group_copies:
        copy.wait_recv()
    other_sums = jnp.transpose(groups_ref[...])[:vectors]
    down_here = down_here + three(nn, split(other_sums), group_map)
    down_parts = split(down_here)
    lanes3 = iota((vectors, LANES), 1)
    middle = (lanes3 >= RANK) & (lanes3 < 2 * RANK)
    down3 = jnp.where(middle, down_parts[1].astype(F32), down_parts[0].astype(F32))
    down3 = down3[:, : 3 * RANK].astype(BF16)
    for j in range(leaf_blocks):
        cut = slice(j * width, (j + 1) * width)
        out_ref[:, cut] = out_ref[:, cut] + nn(down3, final_ref[:, cut])

    for copy in member_copies + side_copies + group_copies:
        copy.wait_send()


def split_lon(n_lon):
    members = 16 if n_lon >= 128 else 1 << n_lon.bit_length() // 2
    return n_lon // members, members


def shards(
    n_lat,
    n_lon,
    ensemble,
    leaf_basis,
    near_blocks,
    local_transfer,
    local_coupling,
    upper_transfer,
    upper_coupling,
    pair_source,
    pair_target,
    pair_coupling,
):
    vectors, points = ensemble.shape
    leaves, leaf_points, window = near_blocks.shape
    halo = window // 2 - leaf_points // 2
    groups, members = split_lon(n_lon)
    pairs = pair_source.shape[2]

    def by_node(matrices):
        nodes = matrices.shape[1]
        return jnp.transpose(matrices[0], (1, 2, 0)).reshape(RANK * RANK, nodes)

    member_blocks = max(1, 2 * members // NODES)
    group_blocks = max(1, 2 * groups // NODES)
    blocks = 2 * leaves // NODES + member_blocks + group_blocks
    upper_nodes = upper_transfer.shape[1]
    operands = (
        ensemble,
        leaf_basis,
        near_blocks,
        by_node(local_transfer),
        by_node(local_coupling),
        by_node(upper_transfer),
        by_node(upper_coupling),
        pair_source[0],
        pair_target[0],
        by_node(pair_coupling[0]),
    )
    return pl.pallas_call(
        functools.partial(kernel, (n_lat, groups, members)),
        out_shape=jax.ShapeDtypeStruct((vectors, points), F32),
        in_specs=[pl.BlockSpec(memory_space=pl.ANY)] * len(operands),
        out_specs=pl.BlockSpec(memory_space=pltpu.VMEM),
        scratch_shapes=[
            pltpu.VMEM((vectors, points + 2 * halo), BF16),
            pltpu.VMEM((RANK, points), BF16),
            pltpu.VMEM(near_blocks.shape, BF16),
            pltpu.VMEM((RANK * RANK, 2 * leaves), F32),
            pltpu.VMEM((RANK * RANK, 2 * leaves), F32),
            pltpu.VMEM((RANK * RANK, upper_nodes), F32),
            pltpu.VMEM((RANK * RANK, upper_nodes), F32),
            pltpu.VMEM((1, pairs), jnp.int32),
            pltpu.VMEM((1, pairs), jnp.int32),
            pltpu.VMEM((RANK * RANK, pairs), F32),
            pltpu.VMEM((blocks * LANES, LANES), BF16),
            pltpu.VMEM((blocks * LANES, LANES), BF16),
            pltpu.VMEM((blocks * LANES, LANES), BF16),
            pltpu.VMEM((blocks * LANES, LANES), BF16),
            pltpu.VMEM((leaves // NODES, LANES, NODES * leaf_points), BF16),
            pltpu.VMEM((3 * leaves, RANK * vectors), F32),
            pltpu.VMEM((members * RANK, LANES), F32),
            pltpu.VMEM((groups * RANK, LANES), F32),
            pltpu.VMEM((3 * RANK, points), BF16),
            pltpu.SemaphoreType.DMA((len(operands),)),
            pltpu.SemaphoreType.DMA((members + groups + 2,)),
            pltpu.SemaphoreType.DMA((members - 1,)),
            pltpu.SemaphoreType.DMA((groups - 1,)),
            pltpu.SemaphoreType.DMA((4,)),
        ],
        compiler_params=pltpu.CompilerParams(
            collective_id=0, has_side_effects=True, vmem_limit_bytes=60 * 2**20
        ),
        name="h2_matvec",
    )(*operands)


def solution(mesh):
    return jax.shard_map(
        functools.partial(shards, mesh.shape["lat"], mesh.shape["lon"]),
        mesh=mesh,
        in_specs=(
            P(None, ("lat", "lon")),
            P(None, ("lat", "lon")),
            P(("lat", "lon"), None, None),
            P(("lat", "lon"), None, None, None),
            P(("lat", "lon"), None, None, None),
            P("lat", None, None, None),
            P("lat", None, None, None),
            P("lat", "lon", None),
            P("lat", "lon", None),
            P("lat", "lon", None, None, None),
        ),
        out_specs=P(None, ("lat", "lon")),
        check_vma=False,
    )
```

time: 154 us -> 38.3 us (0.25)
  the two profiles are of different devices: /device:TPU:8 before, /device:TPU:1 now
where the time goes in v1:
time: 38.3 us; the launch traced here: 38.1 us
  Pallas kernels  36.2 us (95%)
  local copies, waits for them, and re-layouts  1.87 us (5%)
    pallas_call x1, Pallas kernels, shards(): pl.pallas_call(functools.partial(kernel, (n_lat, groups, members)), out_s...  36.2 us
    unnamed x1, local copies, waits for them, and re-layouts  1.87 us

profile of v1, /device:TPU:1, one launch (start us, length us, event | category | flops | bytes accessed | tf_op | source)
XLA Modules:
  0.0 38.1 jit_solution(6203271198648887495)
XLA Ops:
  0.0 36.2 %h2_matvec.1 = f32[64,2048]{1,0:T(8,128)} custom-call(bf16[64,2048]{1,0:T(8,128)(2,1)} %ensemble.1, bf16[16,2048]{1,0:T(8,128)(2,1)} %basis.1, bf16[32,64,320]{2,1,0:T(8,128)(2,1)} %near.1, f32[256,64]{1,0:T(8,128)} %bitcast.29, f32[256,64]{1,0:T(8,128)} %bitcast.30, f32[256,256]{1,0:T(8,128)} %bitcast.27, f32[256,256]{1,0:T(8,128)} %bitcast.28, ...), custom_call_target="tpu_custom_call" | custom-call | tf_op jit(solution)/shard_map/h2_matvec/pallas_call | solution.py:544
  36.2 1.9 %copy.12 = f32[64,2048]{1,0:T(8,128)} copy(f32[64,2048]{1,0:T(8,128)} %h2_matvec.1) | data formatting | bytes 1048576

commit v2 on v1

--- a/solution.py
+++ b/solution.py
@@ -162,7 +162,9 @@
     source,
     target,
     pair_link,
-    out_ref,
+    acc_ref,
+    final_ref,
+    down_ref,
     x_ref,
     basis_ref,
     near_ref,
@@ -178,10 +180,15 @@
     vh_ref,
     vl_ref,
     basis_blocks,
+    across_ref,
     ext_ref,
     members_ref,
     groups_ref,
-    final_ref,
+    to_group_ref,
+    map_ref,
+    local_down_ref,
+    pair_high_ref,
+    pair_low_ref,
     load_sem,
     send_sem,
     member_sem,
@@ -195,19 +202,20 @@
     leaf_points = near.shape[1]
     halo = near.shape[2] // 2 - leaf_points // 2
     lat, lon = lax.axis_index("lat"), lax.axis_index("lon")
-    group, member = lon // members, lon % members
+    group, member = lon // members, lax.rem(lon, members)
     flat = lat * n_lon + lon
     total = n_lat * n_lon
 
-    def at(index):
-        index = lax.rem(index, total)
-        return (index // n_lon, lax.rem(index, n_lon))
-
     member_peers = [(lat, group * members + lax.rem(member + j, members)) for j in range(1, members)]
     group_peers = [(lat, lax.rem(group + j, groups) * members + member) for j in range(1, groups)]
-    above = (lax.rem(lat + 1, n_lat), lon)
-    below = (lax.rem(lat + n_lat - 1, n_lat), lon)
-    after, before = at(flat + 1), at(flat + total - 1)
+    after, before = flat < total - 1, flat > 0
+    above, below = lat < n_lat - 1, lat > 0
+    sides = [
+        (after, ((flat + 1) // n_lon, lax.rem(flat + 1, n_lon))),
+        (before, ((flat - 1) // n_lon, lax.rem(flat + total - 1, n_lon))),
+        (above, (lat + 1, lon)),
+        (below, (lat - 1, lon)),
+    ]
 
     own_points = x_ref.at[:, halo : halo + points]
     loads = [
@@ -231,9 +239,13 @@
         load.start()
 
     barrier = pltpu.get_barrier_semaphore()
-    peers = member_peers + group_peers + [above, below, after, before]
-    for peer in peers:
+    for peer in member_peers + group_peers:
         pl.semaphore_signal(barrier, inc=1, device_id=peer, device_id_type=MESH)
+    for there, peer in sides:
+
+        @pl.when(there)
+        def _():
+            pl.semaphore_signal(barrier, inc=1, device_id=peer, device_id_type=MESH)
 
     row, lane = iota((LANES, LANES), 0), iota((LANES, LANES), 1)
     offset = row - lane // NODES
@@ -271,10 +283,9 @@
     group_base = local_blocks + member_blocks
     group_e, group_v = reader(edges, group_base), reader(links, group_base)
 
-    loads[0].wait()
+    for load in loads[:3]:
+        load.wait()
     operators(turned(le_ref, eye), local_masks[0], edges, 0, spread)
-
-    loads[1].wait()
     width = NODES * leaf_points
     leaf_blocks = leaves // NODES
     keep = iota((NODES, width), 0) == iota((NODES, width), 1) // leaf_points
@@ -286,11 +297,72 @@
                 for s in range(2)
             ]
             basis_blocks[j, k * NODES : (k + 2) * NODES, :] = jnp.concatenate(tiles, axis=0).astype(BF16)
-    loads[2].wait()
-    sums_across = []
+    across = []
     for j in range(leaf_blocks):
         x_part = x_ref[:, halo + j * width : halo + (j + 1) * width]
-        sums_across.append(nt(x_part, basis_blocks[j]))
+        across.append(nt(x_part, basis_blocks[j]))
+        across_ref[:, j * LANES : (j + 1) * LANES] = across[j]
+    start = one_hot(iota((RANK, LANES), 1) == iota((RANK, LANES), 0) * NODES + 1)
+    top = picks(nt, start, local_e(0, 1))
+    top = three(nt, split(top), local_e(0, 1))
+    top = three(nt, split(top), local_e(1, 1))
+    halves = [
+        three(nn, split(side_by_side([across[2 * i], across[2 * i + 1]])), local_e(leaf_blocks + 2 * i, 2))
+        for i in range(leaf_blocks // 2)
+    ]
+    eighth = three(nn, split(side_by_side(halves)), local_e(2, 2))
+    device_sum = three(nt, split(top), split(eighth))
+    empty = jnp.zeros((RANK, LANES - vectors), F32)
+    own_member = members_ref.at[pl.ds(member * RANK, RANK)]
+    own_member[...] = side_by_side([device_sum, empty])
+
+    def copy_to(src, dst, index, arrived, peer):
+        return pltpu.make_async_remote_copy(
+            src_ref=src,
+            dst_ref=dst,
+            send_sem=send_sem.at[index],
+            recv_sem=arrived,
+            device_id=peer,
+            device_id_type=MESH,
+        )
+
+    own_sums = ext_ref.at[leaves : 2 * leaves]
+    first_halo, last_halo = x_ref.at[:, halo : 2 * halo], x_ref.at[:, points : points + halo]
+    left_halo, right_halo = x_ref.at[:, 0:halo], x_ref.at[:, halo + points : points + 2 * halo]
+    below_sums, above_sums = ext_ref.at[0:leaves], ext_ref.at[2 * leaves : 3 * leaves]
+    member_copies = [
+        copy_to(own_member, own_member, j, member_sem.at[j], peer) for j, peer in enumerate(member_peers)
+    ]
+    used = len(member_peers)
+    side_copies = [
+        copy_to(src, dst, used + i, side_sem.at[i], sides[i][1])
+        for i, (src, dst) in enumerate(
+            [
+                (last_halo, left_halo),
+                (first_halo, right_halo),
+                (own_sums, below_sums),
+                (own_sums, above_sums),
+            ]
+        )
+    ]
+    used += 4
+    own_group = groups_ref.at[pl.ds(group * RANK, RANK)]
+    group_copies = [
+        copy_to(own_group, own_group, used + j, group_sem.at[j], peer) for j, peer in enumerate(group_peers)
+    ]
+
+    def exchange():
+        count = len(member_peers) + len(group_peers)
+        for there, _ in sides:
+            count = count + jnp.where(there, 1, 0)
+        pl.semaphore_wait(barrier, count)
+        for copy in member_copies:
+            copy.start()
+        for (there, _), copy in zip(sides, side_copies):
+            pl.when(there)(copy.start)
+
+    for j in range(leaf_blocks):
+        x_part = x_ref[:, halo + j * width : halo + (j + 1) * width]
         by_rank = nt(basis_blocks[j], x_part)
         for k in range(RANK // 2):
             ext_ref[leaves + j * NODES : leaves + (j + 1) * NODES, k * LANES : (k + 1) * LANES] = side_by_side(
@@ -300,45 +372,8 @@
                 ]
             )
 
-    local_ups = climb(sums_across, leaves, local_e)
-    local_paths = paths(leaves, local_e)
-    device_sum = three(nt, split(local_paths[0][0]), split(local_ups[1]))
-    empty = jnp.zeros((RANK, LANES - vectors), F32)
-    own_member = members_ref.at[pl.ds(member * RANK, RANK)]
-    own_member[...] = side_by_side([device_sum, empty])
-
-    pl.semaphore_wait(barrier, len(peers))
-
-    def send(src, dst, index, arrived, peer):
-        copy = pltpu.make_async_remote_copy(
-            src_ref=src,
-            dst_ref=dst,
-            send_sem=send_sem.at[index],
-            recv_sem=arrived,
-            device_id=peer,
-            device_id_type=MESH,
-        )
-        copy.start()
-        return copy
-
-    member_copies = [
-        send(own_member, own_member, j, member_sem.at[j], peer) for j, peer in enumerate(member_peers)
-    ]
-    used = len(member_peers)
-    own_sums = ext_ref.at[leaves : 2 * leaves]
-    side_copies = [
-        send(x_ref.at[:, points : points + halo], x_ref.at[:, 0:halo], used, side_sem.at[0], after),
-        send(
-            x_ref.at[:, halo : 2 * halo],
-            x_ref.at[:, halo + points : points + 2 * halo],
-            used + 1,
-            side_sem.at[1],
-            before,
-        ),
-        send(own_sums, ext_ref.at[0:leaves], used + 2, side_sem.at[2], above),
-        send(own_sums, ext_ref.at[2 * leaves : 3 * leaves], used + 3, side_sem.at[3], below),
-    ]
-    used += 4
+    soon = (lat > 0) | (lon == 0)
+    pl.when(soon)(exchange)
 
     member_slots, group_slots = member_blocks * NODES, group_blocks * NODES
     upper_rows = member_slots + group_slots
@@ -350,43 +385,33 @@
     wanted = jnp.where(slot < member_slots, slot + (groups + group - 1) * scale, slot - member_slots)
     chosen = one_hot(wanted == iota((upper_rows, upper_nodes), 1))
     upper_masks = masks(upper_rows, lambda r: jnp.where(r < member_slots, r, r - member_slots))
-    loads[4].wait()
+    for load in loads[3:]:
+        load.wait()
     operators(turned(ue_ref, chosen), upper_masks[0], edges, local_blocks, spread)
-
+    operators(turned(ul_ref, chosen), upper_masks[1], links, local_blocks, spread)
+    operators(turned(ll_ref, eye), local_masks[1], links, 0, spread)
+
+    per_block = min(members, NODES) * RANK
     member_order = stacked(members)
     member_paths = paths(members, member_e)[-1]
-    to_group = [split(picked_by(nt, split(block), member_order)) for block in member_paths]
-
-    loads[3].wait()
-    operators(turned(ll_ref, eye), local_masks[1], links, 0, spread)
-    loads[5].wait()
-    operators(turned(ul_ref, chosen), upper_masks[1], links, local_blocks, spread)
-
-    for copy in member_copies:
-        copy.wait_recv()
-    member_sums = members_ref[...]
-    member_parts = split(member_sums)
-    per_block = min(members, NODES) * RANK
-    group_sum = None
-    for i, block in enumerate(to_group):
+    for i, block in enumerate(member_paths):
         cut = slice(i * per_block, (i + 1) * per_block)
-        term = three(nn, block, (member_parts[0][cut], member_parts[1][cut]))
-        group_sum = term if group_sum is None else group_sum + term
-    own_group = groups_ref.at[pl.ds(group * RANK, RANK)]
-    own_group[...] = group_sum
-
-    group_copies = [
-        send(own_group, own_group, used + j, group_sem.at[j], peer) for j, peer in enumerate(group_peers)
-    ]
+        high, low = split(picked_by(nt, split(block), member_order))
+        to_group_ref[0:RANK, cut] = high
+        to_group_ref[RANK : 2 * RANK, cut] = low
 
     repeat = iota((LANES, LANES), 1)
     rank_lane = jnp.where(repeat < 3 * RANK, repeat % RANK, -1)
-    own_slots = []
-    for i in range(len(member_paths)):
-        mine = member - i * NODES if members >= NODES else member + members
-        own_slots.append(one_hot((row // NODES == rank_lane) & (row % NODES == mine)))
+
+    def own_slots():
+        picks_own = []
+        for i in range(len(member_paths)):
+            mine = member - i * NODES if members >= NODES else member + members
+            picks_own.append(one_hot((row // NODES == rank_lane) & (row % NODES == mine)))
+        return picks_own
+
     own_path = None
-    for block, pick in zip(member_paths, own_slots):
+    for block, pick in zip(member_paths, own_slots()):
         term = picked_by(nn, split(block), pick)
         own_path = term if own_path is None else own_path + term
     group_slot = group if groups >= NODES else group + groups
@@ -396,68 +421,77 @@
     )
     lifted = split(picks(nn, lift, split(own_path)))
     group_ups = climb([stacked(groups).astype(F32)], groups, group_e)
-    group_map = descend(group_ups, groups, group_e, group_v)[0]
-    group_map = split(three(nn, split(group_map), lifted))
-
-    member_across = []
-    turned_sums = jnp.transpose(member_sums)[:vectors]
-    for i in range(len(member_paths)):
-        part = split(turned_sums[:, i * per_block : (i + 1) * per_block])
-        member_across.append(picked_by(nn, part, member_order))
-    member_ups = climb(member_across, members, member_e)
-    down_here = None
-    for block, pick in zip(descend(member_ups, members, member_e, member_v), own_slots):
-        term = picked_by(nn, split(block), pick)
-        down_here = term if down_here is None else down_here + term
-
-    for j in range(leaf_blocks):
-        folded = split(picked_by(nn, split(local_paths[-1][j]), basis_blocks[j]))
+    group_map = split(three(nn, split(descend(group_ups, groups, group_e, group_v)[0]), lifted))
+    map_ref[0] = group_map[0]
+    map_ref[1] = group_map[1]
+
+    local_ups = climb([across_ref[:, j * LANES : (j + 1) * LANES] for j in range(leaf_blocks)], leaves, local_e)
+    for j, block in enumerate(descend(local_ups, leaves, local_e, local_v)):
+        local_down_ref[:, j * LANES : (j + 1) * LANES] = block
+    for j, block in enumerate(paths(leaves, local_e)[-1]):
+        folded = split(picked_by(nn, split(block), basis_blocks[j]))
         cut = slice(j * width, (j + 1) * width)
         final_ref[0:RANK, cut] = folded[0]
         final_ref[RANK : 2 * RANK, cut] = folded[0]
         final_ref[2 * RANK : 3 * RANK, cut] = folded[1]
 
-    local_down = descend(local_ups, leaves, local_e, local_v)
-
-    loads[9].wait()
-    side_copies[0].wait_recv()
-    side_copies[1].wait_recv()
-
-    @pl.when(flat == 0)
-    def _():
-        x_ref[:, 0:halo] = jnp.zeros((vectors, halo), BF16)
-
-    @pl.when(flat == total - 1)
-    def _():
-        x_ref[:, halo + points :] = jnp.zeros((vectors, halo), BF16)
-
     blank = jnp.zeros((leaf_points, leaf_points), BF16)
     pair_points = 2 * leaf_points
     span = near.shape[2] + leaf_points
-    for j in range(leaves // 2):
+
+    def near_part(j):
         first = side_by_side([near_ref[2 * j], blank])
         second = side_by_side([blank, near_ref[2 * j + 1]])
         weights = jnp.concatenate([first, second], axis=0)
         window = x_ref[:, j * pair_points : j * pair_points + span]
-        out_ref[:, j * pair_points : (j + 1) * pair_points] = nt(window, weights)
-
-    for load in loads[6:9]:
-        load.wait()
-    side_copies[2].wait_recv()
-    side_copies[3].wait_recv()
+        acc_ref[:, j * pair_points : (j + 1) * pair_points] = nt(window, weights)
+
+    for j in range(1, leaves // 2 - 1):
+        near_part(j)
+
     pairs = source.shape[1]
-    spot = iota((3 * leaves, pairs), 0)
-    inside = ((spot >= leaves) | (lat > 0)) & ((spot < 2 * leaves) | (lat < n_lat - 1))
-    reads = jnp.where((spot == src_ref[...]) & inside, 1.0, 0.0)
-    reads = jnp.transpose(reads).astype(BF16)
-    found = [nn(reads, part) for part in split(ext_ref[...])]
     half = RANK // 2
     wide_target = side_by_side([tgt_ref[...], tgt_ref[...]])
     hits = jnp.where(iota((leaves, 2 * pairs), 0) == wide_target, 1.0, 0.0)
     link_rows = pl_ref[...].reshape(RANK, 2, half, pairs)
     link_rows = jnp.concatenate([link_rows[:, 0], link_rows[:, 1]], axis=2)
     link_high = link_rows.astype(BF16).astype(F32)
-    link_parts = (link_high, link_rows - link_high)
+    for ref, part in ((pair_high_ref, link_high), (pair_low_ref, link_rows - link_high)):
+        for j in range(leaf_blocks):
+            hit = hits[j * NODES : (j + 1) * NODES]
+            for k in range(half):
+                ref[j * LANES : (j + 1) * LANES, k * LANES : (k + 1) * LANES] = jnp.concatenate(
+                    [hit * part[a, k : k + 1] for a in range(RANK)], axis=0
+                ).astype(BF16)
+
+    pl.when(jnp.logical_not(soon))(exchange)
+
+    for (there, _), copy in zip([sides[1], sides[0], sides[3], sides[2]], side_copies):
+        pl.when(there)(copy.wait_recv)
+
+    @pl.when(jnp.logical_not(before))
+    def _():
+        x_ref[:, 0:halo] = jnp.zeros((vectors, halo), BF16)
+
+    @pl.when(jnp.logical_not(after))
+    def _():
+        x_ref[:, halo + points :] = jnp.zeros((vectors, halo), BF16)
+
+    @pl.when(jnp.logical_not(below))
+    def _():
+        below_sums[...] = jnp.zeros(below_sums.shape, F32)
+
+    @pl.when(jnp.logical_not(above))
+    def _():
+        above_sums[...] = jnp.zeros(above_sums.shape, F32)
+
+    near_part(0)
+    near_part(leaves // 2 - 1)
+
+    spot = iota((3 * leaves, pairs), 0)
+    reads = jnp.where(spot == src_ref[...], 1.0, 0.0)
+    reads = jnp.transpose(reads).astype(BF16)
+    found = [nn(reads, part) for part in split(ext_ref[...])]
     rights = [[], []]
     for k in range(half):
         for s in range(2):
@@ -465,35 +499,62 @@
             rights[s].append(jnp.concatenate([tile[:, :vectors], tile[:, vectors:]], axis=0))
     rights = [jnp.concatenate(r, axis=0).astype(BF16) for r in rights]
     for j in range(leaf_blocks):
-        hit = hits[j * NODES : (j + 1) * NODES]
-        lefts = []
-        for part in link_parts:
-            columns = []
-            for k in range(half):
-                columns.append(
-                    jnp.concatenate([hit * part[a, k : k + 1] for a in range(RANK)], axis=0).astype(BF16)
-                )
-            lefts.append(side_by_side(columns))
-        added = three(nn, lefts, rights)
-        down = local_down[j] + jnp.transpose(added)
+        block = slice(j * LANES, (j + 1) * LANES)
+        added = three(nn, (pair_high_ref[block, :], pair_low_ref[block, :]), rights)
+        down = local_down_ref[:, block] + jnp.transpose(added)
         cut = slice(j * width, (j + 1) * width)
-        out_ref[:, cut] = out_ref[:, cut] + picked_by(nn, split(down), basis_blocks[j])
+        acc_ref[:, cut] = acc_ref[:, cut] + picked_by(nn, split(down), basis_blocks[j])
+
+    for copy in member_copies:
+        copy.wait_recv()
+    member_sums = members_ref[...]
+    own_group[...] = three(nn, (to_group_ref[0:RANK, :], to_group_ref[RANK : 2 * RANK, :]), split(member_sums))
+
+    @pl.when(lon >= 0)
+    def _():
+        for copy in group_copies:
+            copy.start()
+
+    member_across = []
+    turned_sums = jnp.transpose(members_ref[...])[:vectors]
+    for i in range(len(member_paths)):
+        part = split(turned_sums[:, i * per_block : (i + 1) * per_block])
+        member_across.append(picked_by(nn, part, member_order))
+    member_ups = climb(member_across, members, member_e)
+    down_here = None
+    for block, pick in zip(descend(member_ups, members, member_e, member_v), own_slots()):
+        term = picked_by(nn, split(block), pick)
+        down_here = term if down_here is None else down_here + term
 
     for copy in group_copies:
         copy.wait_recv()
     other_sums = jnp.transpose(groups_ref[...])[:vectors]
-    down_here = down_here + three(nn, split(other_sums), group_map)
+    down_here = down_here + three(nn, split(other_sums), (map_ref[0], map_ref[1]))
     down_parts = split(down_here)
     lanes3 = iota((vectors, LANES), 1)
     middle = (lanes3 >= RANK) & (lanes3 < 2 * RANK)
     down3 = jnp.where(middle, down_parts[1].astype(F32), down_parts[0].astype(F32))
-    down3 = down3[:, : 3 * RANK].astype(BF16)
-    for j in range(leaf_blocks):
+    down_ref[...] = down3.astype(BF16)
+
+    for copy in member_copies + group_copies:
+        copy.wait_send()
+    for (there, _), copy in zip(sides, side_copies):
+        pl.when(there)(copy.wait_send)
+
+
+def last_part(acc_ref, final_ref, down_ref, out_ref, held_ref, sems):
+    down3 = down_ref[:, : 3 * RANK]
+    points = out_ref.shape[1]
+    width = points // 4
+    copies = []
+    for j in range(4):
         cut = slice(j * width, (j + 1) * width)
-        out_ref[:, cut] = out_ref[:, cut] + nn(down3, final_ref[:, cut])
-
-    for copy in member_copies + side_copies + group_copies:
-        copy.wait_send()
+        held_ref[:, cut] = acc_ref[:, cut] + nn(down3, final_ref[:, cut])
+        copy = pltpu.make_async_copy(held_ref.at[:, cut], out_ref.at[:, cut], sems.at[j])
+        copy.start()
+        copies.append(copy)
+    for copy in copies:
+        copy.wait()
 
 
 def split_lon(n_lon):
@@ -541,31 +602,44 @@
         pair_target[0],
         by_node(pair_coupling[0]),
     )
-    return pl.pallas_call(
+    scratch = [
+        ((vectors, points + 2 * halo), BF16),
+        ((RANK, points), BF16),
+        (near_blocks.shape, BF16),
+        ((RANK * RANK, 2 * leaves), F32),
+        ((RANK * RANK, 2 * leaves), F32),
+        ((RANK * RANK, upper_nodes), F32),
+        ((RANK * RANK, upper_nodes), F32),
+        ((1, pairs), jnp.int32),
+        ((1, pairs), jnp.int32),
+        ((RANK * RANK, pairs), F32),
+        ((blocks * LANES, LANES), BF16),
+        ((blocks * LANES, LANES), BF16),
+        ((blocks * LANES, LANES), BF16),
+        ((blocks * LANES, LANES), BF16),
+        ((leaves // NODES, LANES, NODES * leaf_points), BF16),
+        ((vectors, leaves * RANK), F32),
+        ((3 * leaves, RANK * vectors), F32),
+        ((members * RANK, LANES), F32),
+        ((groups * RANK, LANES), F32),
+        ((2 * RANK, members * RANK), BF16),
+        ((2, groups * RANK, LANES), BF16),
+        ((vectors, leaves * RANK), F32),
+        ((leaves * RANK, 2 * pairs * RANK // 2), BF16),
+        ((leaves * RANK, 2 * pairs * RANK // 2), BF16),
+    ]
+    whole = pl.BlockSpec(memory_space=pltpu.VMEM)
+    kept = pl.pallas_call(
         functools.partial(kernel, (n_lat, groups, members)),
-        out_shape=jax.ShapeDtypeStruct((vectors, points), F32),
-        in_specs=[pl.BlockSpec(memory_space=pl.ANY)] * len(operands),
-        out_specs=pl.BlockSpec(memory_space=pltpu.VMEM),
-        scratch_shapes=[
-            pltpu.VMEM((vectors, points + 2 * halo), BF16),
-            pltpu.VMEM((RANK, points), BF16),
-            pltpu.VMEM(near_blocks.shape, BF16),
-            pltpu.VMEM((RANK * RANK, 2 * leaves), F32),
-            pltpu.VMEM((RANK * RANK, 2 * leaves), F32),
-            pltpu.VMEM((RANK * RANK, upper_nodes), F32),
-            pltpu.VMEM((RANK * RANK, upper_nodes), F32),
-            pltpu.VMEM((1, pairs), jnp.int32),
-            pltpu.VMEM((1, pairs), jnp.int32),
-            pltpu.VMEM((RANK * RANK, pairs), F32),
-            pltpu.VMEM((blocks * LANES, LANES), BF16),
-            pltpu.VMEM((blocks * LANES, LANES), BF16),
-            pltpu.VMEM((blocks * LANES, LANES), BF16),
-            pltpu.VMEM((blocks * LANES, LANES), BF16),
-            pltpu.VMEM((leaves // NODES, LANES, NODES * leaf_points), BF16),
-            pltpu.VMEM((3 * leaves, RANK * vectors), F32),
-            pltpu.VMEM((members * RANK, LANES), F32),
-            pltpu.VMEM((groups * RANK, LANES), F32),
-            pltpu.VMEM((3 * RANK, points), BF16),
+        out_shape=(
+            jax.ShapeDtypeStruct((vectors, points), F32),
+            jax.ShapeDtypeStruct((3 * RANK, points), BF16),
+            jax.ShapeDtypeStruct((vectors, LANES), BF16),
+        ),
+        in_specs=[pl.BlockSpec(memory_space=pltpu.HBM)] * len(operands),
+        out_specs=(whole, whole, whole),
+        scratch_shapes=[pltpu.VMEM(shape, dtype) for shape, dtype in scratch]
+        + [
             pltpu.SemaphoreType.DMA((len(operands),)),
             pltpu.SemaphoreType.DMA((members + groups + 2,)),
             pltpu.SemaphoreType.DMA((members - 1,)),
@@ -573,10 +647,19 @@
             pltpu.SemaphoreType.DMA((4,)),
         ],
         compiler_params=pltpu.CompilerParams(
-            collective_id=0, has_side_effects=True, vmem_limit_bytes=60 * 2**20
+            collective_id=0, has_side_effects=True, vmem_limit_bytes=40 * 2**20
         ),
-        name="h2_matvec",
-    )(*operands)
+        name="h2_tree",
+    )(*[pltpu.with_memory_space_constraint(operand, pltpu.HBM) for operand in operands])
+    return pl.pallas_call(
+        last_part,
+        out_shape=jax.ShapeDtypeStruct((vectors, points), F32),
+        in_specs=[whole] * 3,
+        out_specs=pl.BlockSpec(memory_space=pltpu.HBM),
+        scratch_shapes=[pltpu.VMEM((vectors, points), F32), pltpu.SemaphoreType.DMA((4,))],
+        compiler_params=pltpu.CompilerParams(vmem_limit_bytes=8 * 2**20),
+        name="h2_last",
+    )(*kept)
 
 
 def solution(mesh):

time: 38.3 us -> 30.3 us (0.79)
  Pallas kernels: 36.2 us -> 30.2 us
  local copies, waits for them, and re-layouts: 1.87 us -> 0 us
    pallas_call x1, Pallas kernels: 36.2 us -> 29.2 us  [shards(): pl.pallas_call(functools.partial(kernel, (n_lat, groups, members)), out_s...]
    unnamed x1 -> x0, local copies, waits for them, and re-layouts: 1.87 us -> none
    pallas_call x0 -> x1, Pallas kernels: none -> 0.96 us  [shards(): pl.pallas_call(last_part, out_shape=jax.ShapeDtypeStruct((vectors, points...]
where the time goes in v2:
time: 30.3 us; the launch traced here: 30.2 us
  Pallas kernels  30.2 us (100%)
    pallas_call x1, Pallas kernels, shards(): pl.pallas_call(functools.partial(kernel, (n_lat, groups, members)), out_s...  29.2 us
    pallas_call x1, Pallas kernels, shards(): pl.pallas_call(last_part, out_shape=jax.ShapeDtypeStruct((vectors, points...  0.96 us

profile of v2, /device:TPU:1, one launch (start us, length us, event | category | flops | bytes accessed | tf_op | source)
XLA Modules:
  0.0 30.2 jit_solution(6085641123226160989)
XLA Ops:
  0.0 29.2 %h2_tree.1 = (f32[64,2048]{1,0:T(8,128)S(1)}, bf16[48,2048]{1,0:T(8,128)(2,1)S(1)}, bf16[64,128]{1,0:T(8,128)(2,1)S(1)}) custom-call(bf16[64,2048]{1,0:T(8,128)(2,1)} %ensemble.1, bf16[16,2048]{1,0:T(8,128)(2,1)} %basis.1, bf16[32,64,320]{2,1,0:T(8,128)(2,1)} %near.1, f32[256,64]{1,0:T(8,128)} %bitcast.29, f32[256,64]{1,0:T(8,128)} %bitcast.30, ...), custom_call_target="tpu_custom_call" | custom-call | tf_op jit(solution)/shard_map/h2_tree/pallas_call | solution.py:632
  29.2 1.0 %h2_last.1 = f32[64,2048]{1,0:T(8,128)} custom-call(f32[64,2048]{1,0:T(8,128)S(1)} %get-tuple-element.8.acc_ref, bf16[48,2048]{1,0:T(8,128)(2,1)S(1)} %get-tuple-element.9.final_ref, bf16[64,128]{1,0:T(8,128)(2,1)S(1)} %get-tuple-element.10.down_ref), custom_call_target="tpu_custom_call" | custom-call | tf_op jit(solution)/shard_map/h2_last/pallas_call | solution.py:654

commit v3 on v2

v3 whole, which is shorter than its diff:
```python
import functools

import jax
import jax.numpy as jnp
from jax import lax
from jax.experimental import pallas as pl
from jax.experimental.pallas import tpu as pltpu
from jax.sharding import PartitionSpec as P

F32 = jnp.float32
BF16 = jnp.bfloat16
RANK = 16
LANES = 128
NODES = 8
MESH = pl.DeviceIdType.MESH


def iota(shape, axis):
    return lax.broadcasted_iota(jnp.int32, shape, axis)


def one_hot(mask):
    return jnp.where(mask, 1.0, 0.0).astype(BF16)


def nn(a, b):
    return lax.dot_general(a, b, (((1,), (0,)), ((), ())), preferred_element_type=F32)


def nt(a, b):
    return lax.dot_general(a, b, (((1,), (1,)), ((), ())), preferred_element_type=F32)


def split(x):
    high = x.astype(BF16)
    return high, (x - high.astype(F32)).astype(BF16)


def three(dot, a, b):
    rows = a[0].shape[0]
    both = dot(jnp.concatenate(a, axis=0), b[0])
    return both[:rows] + (both[rows:] + dot(a[0], b[1]))


def picked_by(dot, a, b):
    rows = a[0].shape[0]
    both = dot(jnp.concatenate(a, axis=0), b)
    return both[:rows] + both[rows:]


def picks(dot, a, b):
    return dot(a, b[0]) + dot(a, b[1])


def side_by_side(parts):
    return jnp.concatenate(parts, axis=1)


def rows_of(refs, first, count):
    return tuple(ref[pl.ds(first * LANES, count * LANES), :] for ref in refs)


def each(low, high, act):
    def step(index, carry):
        act(index)
        return carry

    lax.fori_loop(low, high, step, 0)


def turn_of(index, count):
    return jnp.where(index <= count // 2, jnp.maximum(2 * index - 1, 0), 2 * (count - index))


def index_at(turn, count):
    return jnp.where(turn % 2 == 1, (turn + 1) // 2, jnp.where(turn == 0, 0, count - turn // 2))


def climb(leaves, count, edge):
    ups = {}
    if count < NODES:
        ups[0] = leaves[0]
        if count >= 4:
            ups[0] = ups[0] + three(nn, split(ups[0]), edge(0, 1))
        return ups
    level = count // NODES
    for i, block in enumerate(leaves):
        ups[level + i] = block
    while level > 1:
        for i in range(level // 2, level):
            pair = side_by_side([ups[2 * i], ups[2 * i + 1]])
            ups[i] = three(nn, split(pair), edge(2 * i, 2))
        level //= 2
    return crown(ups, edge)


def crown(ups, edge):
    ups[0] = three(nn, split(ups[1]), edge(1, 1))
    ups[0] = ups[0] + three(nn, split(ups[0]), edge(0, 1))
    return ups


def descend(ups, count, edge, link, across):
    rows = ups[0].shape[0]
    top = three(across, split(ups[0]), link(0, 1))
    if count >= 4:
        slot = iota((rows, LANES), 1) % NODES
        first = jnp.where((slot == 2) | (slot == 3), top, 0.0)
        top = top + three(nt, split(first), edge(0, 1))
    if count < NODES:
        return [top]
    level = [three(across, split(ups[1]), link(1, 1)) + three(nt, split(top), edge(1, 1))]
    while len(level) < count // NODES:
        width = len(level)
        below = []
        for i, block in enumerate(level):
            node = width + i
            both = three(nt, split(block), edge(2 * node, 2))
            for side in range(2):
                child = 2 * node + side
                own = three(across, split(ups[child]), link(child, 1))
                below.append(own + both[:, side * LANES : (side + 1) * LANES])
        level = below
    return level


def paths(count, edge):
    start = one_hot(iota((RANK, LANES), 1) == iota((RANK, LANES), 0) * NODES + 1)
    step = picks(nt, start, edge(0, 1))
    if count >= 4:
        step = three(nt, split(step), edge(0, 1))
    if count < NODES:
        return [step]
    return longer([three(nt, split(step), edge(1, 1))], count, edge)


def longer(level, count, edge):
    while len(level) < count // NODES:
        below = []
        for i, block in enumerate(level):
            both = three(nt, split(block), edge(2 * (len(level) + i), 2))
            below += [both[:, :LANES], both[:, LANES:]]
        level = below
    return level


def stacked(blocks):
    count = blocks
    members = min(count, NODES)
    offset = count if count < NODES else 0
    row = iota((members * RANK, LANES), 0)
    lane = iota((members * RANK, LANES), 1)
    return one_hot(lane == (row % RANK) * NODES + row // RANK + offset)


def operators(turned, masks, edge_refs, block, spread):
    (high, low), mask = turned, masks
    nodes = high.shape[0]
    for half in range(2):
        cut = slice(half * LANES, (half + 1) * LANES)
        both = jnp.concatenate([high[:, cut], low[:, cut]], axis=0)
        for pair in range(NODES // 2):
            wide = nn(both, spread[pair])
            parts = [
                [
                    jnp.where(mask, wide[k * nodes : (k + 1) * nodes, s * LANES : (s + 1) * LANES], 0.0)
                    for s in range(2)
                ]
                for k in range(2)
            ]
            for k in range(2):
                for j in range(nodes // NODES):
                    rows = slice(j * NODES, (j + 1) * NODES)
                    tile = jnp.concatenate([parts[k][0][rows], parts[k][1][rows]], axis=0)
                    start = (block + j) * LANES + (half * NODES + 2 * pair) * NODES
                    edge_refs[k][start : start + 2 * NODES, :] = tile.astype(BF16)


def kernel(
    sizes,
    ensemble,
    basis,
    near,
    local_edge,
    local_link,
    upper_edge,
    upper_link,
    source,
    target,
    pair_link,
    acc_ref,
    final_ref,
    down_ref,
    x_ref,
    basis_ref,
    near_ref,
    le_ref,
    ll_ref,
    ue_ref,
    ul_ref,
    src_ref,
    tgt_ref,
    pl_ref,
    eh_ref,
    el_ref,
    vh_ref,
    vl_ref,
    basis_blocks,
    ups_ref,
    top_ref,
    ext_ref,
    members_ref,
    groups_ref,
    to_group_ref,
    map_ref,
    local_down_ref,
    pair_high_ref,
    pair_low_ref,
    here_ref,
    load_sem,
    member_send,
    group_send,
    stand_in_send,
    side_send,
    member_sem,
    group_sem,
    side_sem,
    member_in,
    group_in,
    side_in,
):
    n_lat, groups, members = sizes
    n_lon = groups * members
    vectors, points = ensemble.shape
    leaves = near.shape[0]
    leaf_points = near.shape[1]
    halo = near.shape[2] // 2 - leaf_points // 2
    lat, lon = lax.axis_index("lat"), lax.axis_index("lon")
    group, member = lon // members, lax.rem(lon, members)
    flat = lat * n_lon + lon
    total = n_lat * n_lon

    member_shift = jnp.where((lat == 0) & (group == 0), 1, 0)
    group_shift = jnp.where((lat == 0) & (member == 0), 1, 0)
    cores = min(members, 2)
    lines = members // cores
    member_turn = turn_of(member // cores, lines) * cores + lax.rem(member, cores)
    member_turn = lax.rem(member_turn + members - member_shift, members)
    group_turn = lax.rem(turn_of(group, groups) + groups - group_shift, groups)

    def member_by(turn):
        turn = lax.rem(turn + member_shift, members)
        return index_at(turn // cores, lines) * cores + lax.rem(turn, cores)

    def group_by(turn):
        return index_at(lax.rem(turn + group_shift, groups), groups)

    def member_at(j):
        return (lat, group * members + j)

    def group_at(j):
        return (lat, j * members + member)

    after, before = flat < total - 1, flat > 0
    above, below = lat < n_lat - 1, lat > 0
    after_at = ((flat + 1) // n_lon, lax.rem(flat + 1, n_lon))
    before_at = ((flat - 1) // n_lon, lax.rem(flat + total - 1, n_lon))
    above_at, below_at = (lat + 1, lon), (lat - 1, lon)
    earlier = [after & (flat == 0), before & (flat != 1), above & (flat == 0), below & (flat != n_lon)]
    later = [after & (flat != 0), before & (flat == 1), above & (flat != 0), below & (flat == n_lon)]
    beside_at = [after_at, before_at, above_at, below_at]
    mirror = [1, 0, 3, 2]

    own_points = x_ref.at[:, halo : halo + points]
    loads = [
        pltpu.make_async_copy(src, dst, load_sem.at[i])
        for i, (src, dst) in enumerate(
            [
                (local_edge, le_ref),
                (basis, basis_ref),
                (ensemble, own_points),
                (local_link, ll_ref),
                (upper_edge, ue_ref),
                (upper_link, ul_ref),
                (source, src_ref),
                (target, tgt_ref),
                (pair_link, pl_ref),
                (near, near_ref),
            ]
        )
    ]
    for load in loads:
        load.start()

    barrier = pltpu.get_barrier_semaphore()

    def signal(semaphore, peer):
        pl.semaphore_signal(semaphore, inc=1, device_id=peer, device_id_type=MESH)

    each(member_turn + 1, members, lambda t: signal(barrier, member_at(member_by(t))))
    each(group_turn + 1, groups, lambda t: signal(barrier, group_at(group_by(t))))
    for there, peer in zip(later, beside_at):
        pl.when(there)(functools.partial(signal, barrier, peer))
    stand_in = flat == 1
    stood_for = (lat == 0) & (member == 0) & (group > 0)
    pl.when(stood_for)(lambda: signal(barrier, (lat, 1)))

    heard = member_turn + group_turn + jnp.where(stand_in, groups - 1, 0)
    for there in earlier:
        heard = heard + jnp.where(there, 1, 0)
    pl.semaphore_wait(barrier, heard)
    each(0, member_turn, lambda t: signal(member_in.at[member], member_at(member_by(t))))
    each(0, group_turn, lambda t: signal(group_in.at[group], group_at(group_by(t))))
    for k in range(4):
        pl.when(earlier[k])(functools.partial(signal, side_in.at[mirror[k]], beside_at[k]))

    row, lane = iota((LANES, LANES), 0), iota((LANES, LANES), 1)
    offset = row - lane // NODES
    spread = []
    for pair in range(NODES // 2):
        spread.append(
            side_by_side([one_hot(offset == (2 * pair + s) * RANK) for s in range(2)])
        )

    def masks(count, slots):
        node_slot = slots(iota((count, LANES), 0))
        column = iota((count, LANES), 1) % NODES
        inner = node_slot >= 2
        edge = inner & (column == (node_slot // 2) % NODES)
        link = inner & (column == (node_slot + 1 - 2 * (node_slot % 2)) % NODES)
        return edge, link

    eye = one_hot(iota((2 * leaves, 2 * leaves), 0) == iota((2 * leaves, 2 * leaves), 1))
    local_masks = masks(2 * leaves, lambda r: r)

    def turned(ref, chosen):
        parts = split(ref[...])
        return tuple(nt(chosen, part).astype(BF16) for part in parts)

    edges, links = (eh_ref, el_ref), (vh_ref, vl_ref)
    local_blocks = 2 * leaves // NODES
    member_blocks = max(1, 2 * members // NODES)
    group_blocks = max(1, 2 * groups // NODES)

    def reader(refs, base):
        return lambda first, count: rows_of(refs, base + first, count)

    local_e, local_v = reader(edges, 0), reader(links, 0)
    member_e, member_v = reader(edges, local_blocks), reader(links, local_blocks)
    group_base = local_blocks + member_blocks
    group_e, group_v = reader(edges, group_base), reader(links, group_base)

    for load in loads[:3]:
        load.wait()
    operators(turned(le_ref, eye), local_masks[0], edges, 0, spread)
    width = NODES * leaf_points
    leaf_blocks = leaves // NODES
    keep = iota((NODES, width), 0) == iota((NODES, width), 1) // leaf_points
    for j in range(leaf_blocks):
        part = basis_ref[:, j * width : (j + 1) * width].astype(F32)
        for k in range(0, RANK, 2):
            tiles = [
                jnp.where(keep, jnp.broadcast_to(part[k + s : k + s + 1], (NODES, width)), 0.0)
                for s in range(2)
            ]
            basis_blocks[j, k * NODES : (k + 2) * NODES, :] = jnp.concatenate(tiles, axis=0).astype(BF16)
    across = []
    for j in range(leaf_blocks):
        x_part = x_ref[:, halo + j * width : halo + (j + 1) * width]
        across.append(nt(x_part, basis_blocks[j]))
    top = paths(NODES, local_e)[0]
    halves = [
        three(nn, split(side_by_side([across[2 * i], across[2 * i + 1]])), local_e(leaf_blocks + 2 * i, 2))
        for i in range(leaf_blocks // 2)
    ]
    eighth = three(nn, split(side_by_side(halves)), local_e(2, 2))
    device_sum = three(nt, split(top), split(eighth))
    top_ref[...] = top
    for i, block in enumerate([eighth] + halves + across):
        ups_ref[:, i * LANES : (i + 1) * LANES] = block
    empty = jnp.zeros((RANK, LANES - vectors), F32)
    own_member = members_ref.at[pl.ds(member * RANK, RANK)]
    own_member[...] = side_by_side([device_sum, empty])

    def copy_to(src, dst, sent, arrived, peer):
        return pltpu.make_async_remote_copy(
            src_ref=src,
            dst_ref=dst,
            send_sem=sent,
            recv_sem=arrived,
            device_id=peer,
            device_id_type=MESH,
        )

    def member_copy(j):
        return copy_to(own_member, own_member, member_send.at[j], member_sem.at[member], member_at(j))

    def member_arrival(j):
        there = members_ref.at[pl.ds(j * RANK, RANK)]
        return copy_to(there, there, member_send.at[j], member_sem.at[j], member_at(j))

    own_group = groups_ref.at[pl.ds(group * RANK, RANK)]

    def group_copy(j):
        return copy_to(own_group, own_group, group_send.at[j], group_sem.at[group], group_at(j))

    def stand_in_copy(j):
        return copy_to(own_group, own_group, stand_in_send.at[j], group_sem.at[0], (lat, j * members))

    def group_arrival(j):
        there = groups_ref.at[pl.ds(j * RANK, RANK)]
        return copy_to(there, there, group_send.at[j], group_sem.at[j], group_at(j))

    own_sums = ext_ref.at[leaves : 2 * leaves]
    first_halo, last_halo = x_ref.at[:, halo : 2 * halo], x_ref.at[:, points : points + halo]
    left_halo, right_halo = x_ref.at[:, 0:halo], x_ref.at[:, halo + points : points + 2 * halo]
    below_sums, above_sums = ext_ref.at[0:leaves], ext_ref.at[2 * leaves : 3 * leaves]
    to_after = copy_to(last_halo, left_halo, side_send.at[0], side_sem.at[0], after_at)
    to_before = copy_to(first_halo, right_halo, side_send.at[1], side_sem.at[1], before_at)
    to_above = copy_to(own_sums, below_sums, side_send.at[2], side_sem.at[2], above_at)
    to_below = copy_to(own_sums, above_sums, side_send.at[3], side_sem.at[3], below_at)
    from_before, from_after, from_below, from_above = to_after, to_before, to_above, to_below
    side_copies = [to_after, to_before, to_above, to_below]

    def to_member(j):
        pl.semaphore_wait(member_in.at[j], 1)
        member_copy(j).start()

    def to_group(j):
        pl.semaphore_wait(group_in.at[j], 1)
        group_copy(j).start()

    def to_side(k):
        pl.semaphore_wait(side_in.at[k], 1)
        side_copies[k].start()

    each(0, member_turn, lambda t: member_copy(member_by(member_turn - 1 - t)).start())
    for k in range(2):
        pl.when(earlier[k])(side_copies[k].start)

    for j in range(leaf_blocks):
        x_part = x_ref[:, halo + j * width : halo + (j + 1) * width]
        by_rank = nt(basis_blocks[j], x_part)
        for k in range(RANK // 2):
            ext_ref[leaves + j * NODES : leaves + (j + 1) * NODES, k * LANES : (k + 1) * LANES] = side_by_side(
                [
                    by_rank[k * NODES : (k + 1) * NODES],
                    by_rank[(k + RANK // 2) * NODES : (k + RANK // 2 + 1) * NODES],
                ]
            )

    for k in range(2, 4):
        pl.when(earlier[k])(side_copies[k].start)

    member_slots, group_slots = member_blocks * NODES, group_blocks * NODES
    upper_rows = member_slots + group_slots
    upper_nodes = upper_edge.shape[1]
    slot = iota((upper_rows, upper_nodes), 0)
    scale = jnp.where(slot >= 2, 2, 1)
    for power in range(2, members.bit_length()):
        scale = jnp.where(slot >= 2**power, 2**power, scale)
    wanted = jnp.where(slot < member_slots, slot + (groups + group - 1) * scale, slot - member_slots)
    chosen = one_hot(wanted == iota((upper_rows, upper_nodes), 1))
    upper_masks = masks(upper_rows, lambda r: jnp.where(r < member_slots, r, r - member_slots))
    loads[4].wait()
    operators(turned(ue_ref, chosen), upper_masks[0], edges, local_blocks, spread)

    per_block = min(members, NODES) * RANK
    member_order = stacked(members)
    member_paths = paths(members, member_e)
    for i, block in enumerate(member_paths):
        cut = slice(i * per_block, (i + 1) * per_block)
        high, low = split(picked_by(nt, split(block), member_order))
        to_group_ref[0:RANK, cut] = high
        to_group_ref[RANK : 2 * RANK, cut] = low

    blank = jnp.zeros((leaf_points, leaf_points), BF16)
    pair_points = 2 * leaf_points
    span = near.shape[2] + leaf_points
    pairs = source.shape[1]
    half = RANK // 2

    def near_part(j, low, high, add):
        first = side_by_side([near_ref[2 * j], blank])
        second = side_by_side([blank, near_ref[2 * j + 1]])
        weights = jnp.concatenate([first, second], axis=0)[:, low:high]
        window = x_ref[:, j * pair_points + low : j * pair_points + high]
        cut = slice(j * pair_points, (j + 1) * pair_points)
        part = nt(window, weights)
        acc_ref[:, cut] = acc_ref[:, cut] + part if add else part

    def local_work():
        for load in loads[3:4] + loads[5:]:
            load.wait()
        operators(turned(ul_ref, chosen), upper_masks[1], links, local_blocks, spread)
        operators(turned(ll_ref, eye), local_masks[1], links, 0, spread)

        own_rows, own_lanes = iota((RANK, LANES), 0), iota((RANK, LANES), 1)
        starts = []
        for i in range(len(member_paths)):
            mine = member - i * NODES if members >= NODES else member + members
            inside = (mine >= 0) & (mine < NODES)
            starts.append(jnp.where((own_lanes == own_rows * NODES + mine) & inside, 1.0, 0.0))
        member_ups = climb(starts, members, member_e)
        group_slot = group if groups >= NODES else group + groups
        place = one_hot((row // NODES == lane // NODES) & (row % NODES == 1) & (lane % NODES == group_slot))
        placed = picked_by(nn, split(three(nn, split(member_ups[0]), member_e(0, 1))), place)
        group_ups = climb([placed], groups, group_e)
        maps = [
            picked_by(nt, split(block), member_order)
            for block in descend(member_ups, members, member_e, member_v, nn)
        ]
        maps.append(picked_by(nt, split(descend(group_ups, groups, group_e, group_v, nn)[0]), stacked(groups)))
        for i, part in enumerate(split(side_by_side(maps))):
            map_ref[i] = jnp.concatenate([part] * 3, axis=0)

        local_ups = {i + 1: ups_ref[:, i * LANES : (i + 1) * LANES] for i in range(2 * leaf_blocks - 1)}
        for j, block in enumerate(descend(crown(local_ups, local_e), leaves, local_e, local_v, nt)):
            local_down_ref[:, j * LANES : (j + 1) * LANES] = block
        for j, block in enumerate(longer([top_ref[...]], leaves, local_e)):
            folded = split(picked_by(nn, split(block), basis_blocks[j]))
            cut = slice(j * width, (j + 1) * width)
            final_ref[0:RANK, cut] = folded[0]
            final_ref[RANK : 2 * RANK, cut] = folded[0]
            final_ref[2 * RANK : 3 * RANK, cut] = folded[1]

        for j in range(leaves // 2):
            low, high = (halo if j == 0 else 0), (span - halo if j == leaves // 2 - 1 else span)
            near_part(j, low, high, False)

        wide_target = side_by_side([tgt_ref[...], tgt_ref[...]])
        hits = jnp.where(iota((leaves, 2 * pairs), 0) == wide_target, 1.0, 0.0)
        link_rows = pl_ref[...].reshape(RANK, 2, half, pairs)
        link_rows = jnp.concatenate([link_rows[:, 0], link_rows[:, 1]], axis=2)
        link_high = link_rows.astype(BF16).astype(F32)
        for ref, part in ((pair_high_ref, link_high), (pair_low_ref, link_rows - link_high)):
            for j in range(leaf_blocks):
                hit = hits[j * NODES : (j + 1) * NODES]
                for k in range(half):
                    ref[j * LANES : (j + 1) * LANES, k * LANES : (k + 1) * LANES] = jnp.concatenate(
                        [hit * part[a, k : k + 1] for a in range(RANK)], axis=0
                    ).astype(BF16)

    for k in (0, 2):
        pl.when(later[k])(functools.partial(to_side, k))

    def late_sends():
        each(member_turn + 1, members - member_shift, lambda t: to_member(member_by(t)))

    def beside():
        for k in (1, 3):
            pl.when(later[k])(functools.partial(to_side, k))

        pl.when(below)(from_below.wait_recv)
        pl.when(above)(from_above.wait_recv)

        @pl.when(jnp.logical_not(below))
        def _():
            below_sums[...] = jnp.zeros(below_sums.shape, F32)

        @pl.when(jnp.logical_not(above))
        def _():
            above_sums[...] = jnp.zeros(above_sums.shape, F32)

        spot = iota((3 * leaves, pairs), 0)
        reads = jnp.where(spot == src_ref[...], 1.0, 0.0)
        reads = jnp.transpose(reads).astype(BF16)
        found = [nn(reads, part) for part in split(ext_ref[...])]
        left_side = iota((pairs, LANES), 1) < vectors
        rights = []
        for k in range(half):
            high, low = (part[:, k * LANES : (k + 1) * LANES] for part in found)
            rights.append(jnp.where(left_side, high, pltpu.roll(low, vectors, 1)))
            rights.append(jnp.where(left_side, pltpu.roll(high, vectors, 1), low))
        rights = jnp.concatenate(rights, axis=0).astype(BF16)
        for j in range(leaf_blocks):
            block = slice(j * LANES, (j + 1) * LANES)
            high_both = nn(pair_high_ref[block, :], rights)
            added = high_both[:, :vectors] + (high_both[:, vectors:] + nn(pair_low_ref[block, :], rights[:, :vectors]))
            down = local_down_ref[:, block] + jnp.transpose(added)
            cut = slice(j * width, (j + 1) * width)
            acc_ref[:, cut] = acc_ref[:, cut] + picked_by(nn, split(down), basis_blocks[j])

        pl.when(before)(from_before.wait_recv)
        pl.when(after)(from_after.wait_recv)

        @pl.when(jnp.logical_not(before))
        def _():
            left_halo[...] = jnp.zeros((vectors, halo), BF16)

        @pl.when(jnp.logical_not(after))
        def _():
            right_halo[...] = jnp.zeros((vectors, halo), BF16)

        near_part(0, 0, halo, True)
        near_part(leaves // 2 - 1, span - halo, span, True)

    def relay():
        @pl.when((member_shift == 1) & (member_turn < members - 1))
        def _():
            to_member(0)

        each(0, member, lambda j: member_arrival(j).wait_recv())
        each(member + 1, members, lambda j: member_arrival(j).wait_recv())
        own_group[...] = three(
            nn, (to_group_ref[0:RANK, :], to_group_ref[RANK : 2 * RANK, :]), split(members_ref[...])
        )
        @pl.when(flat > 0)
        def _():
            each(0, group_turn, lambda t: group_copy(group_by(group_turn - 1 - t)).start())

        @pl.when(stand_in)
        def _():
            each(1, groups, lambda j: stand_in_copy(j).start())

        each(group_turn + 1, groups, lambda t: to_group(group_by(t)))

    def stage(step, carry):
        turn = jnp.where((lat == 0) | (step == 0), step, 3 - step)
        pl.when(turn == 0)(local_work)
        pl.when(step == 0)(late_sends)
        pl.when(turn == 1)(beside)
        pl.when(turn == 2)(relay)
        return carry

    lax.fori_loop(0, 3, stage, 0)

    def mapped(ref, first, count):
        cut = slice(first * RANK, (first + count) * RANK)
        turned_sums = jnp.transpose(ref[...])[:vectors]
        return three(nt, split(turned_sums), (map_ref[0][:, cut], map_ref[1][:, cut]))

    here_ref[...] = mapped(members_ref, 0, members)
    each(0, group, lambda j: group_arrival(j).wait_recv())
    each(group + 1, groups, lambda j: group_arrival(j).wait_recv())
    down_here = here_ref[...] + mapped(groups_ref, members, groups)
    down_parts = split(down_here)
    lanes3 = iota(down_here.shape, 1)
    middle = (lanes3 >= RANK) & (lanes3 < 2 * RANK)
    down3 = jnp.where(middle, down_parts[1].astype(F32), down_parts[0].astype(F32))
    down_ref[...] = down3.astype(BF16)

    each(0, member, lambda j: member_copy(j).wait_send())
    each(member + 1, members, lambda j: member_copy(j).wait_send())

    @pl.when(flat > 0)
    def _():
        each(0, group, lambda j: group_copy(j).wait_send())
        each(group + 1, groups, lambda j: group_copy(j).wait_send())

    @pl.when(stand_in)
    def _():
        each(1, groups, lambda j: stand_in_copy(j).wait_send())

    pl.when(after)(to_after.wait_send)
    pl.when(before)(to_before.wait_send)
    pl.when(above)(to_above.wait_send)
    pl.when(below)(to_below.wait_send)


def last_part(acc_ref, final_ref, down_ref, out_ref, held_ref, sems):
    down3 = down_ref[...]
    points = out_ref.shape[1]
    width = points // 4
    copies = []
    for j in range(4):
        cut = slice(j * width, (j + 1) * width)
        held_ref[:, cut] = acc_ref[:, cut] + nn(down3, final_ref[:, cut])
        copy = pltpu.make_async_copy(held_ref.at[:, cut], out_ref.at[:, cut], sems.at[j])
        copy.start()
        copies.append(copy)
    for copy in copies:
        copy.wait()


def split_lon(n_lon):
    members = 16 if n_lon >= 128 else 1 << n_lon.bit_length() // 2
    return n_lon // members, members


def shards(
    n_lat,
    n_lon,
    ensemble,
    leaf_basis,
    near_blocks,
    local_transfer,
    local_coupling,
    upper_transfer,
    upper_coupling,
    pair_source,
    pair_target,
    pair_coupling,
):
    vectors, points = ensemble.shape
    leaves, leaf_points, window = near_blocks.shape
    halo = window // 2 - leaf_points // 2
    groups, members = split_lon(n_lon)
    pairs = pair_source.shape[2]

    def by_node(matrices):
        nodes = matrices.shape[1]
        return jnp.transpose(matrices[0], (1, 2, 0)).reshape(RANK * RANK, nodes)

    member_blocks = max(1, 2 * members // NODES)
    group_blocks = max(1, 2 * groups // NODES)
    blocks = 2 * leaves // NODES + member_blocks + group_blocks
    upper_nodes = upper_transfer.shape[1]
    operands = (
        ensemble,
        leaf_basis,
        near_blocks,
        by_node(local_transfer),
        by_node(local_coupling),
        by_node(upper_transfer),
        by_node(upper_coupling),
        pair_source[0],
        pair_target[0],
        by_node(pair_coupling[0]),
    )
    scratch = [
        ((vectors, points + 2 * halo), BF16),
        ((RANK, points), BF16),
        (near_blocks.shape, BF16),
        ((RANK * RANK, 2 * leaves), F32),
        ((RANK * RANK, 2 * leaves), F32),
        ((RANK * RANK, upper_nodes), F32),
        ((RANK * RANK, upper_nodes), F32),
        ((1, pairs), jnp.int32),
        ((1, pairs), jnp.int32),
        ((RANK * RANK, pairs), F32),
        ((blocks * LANES, LANES), BF16),
        ((blocks * LANES, LANES), BF16),
        ((blocks * LANES, LANES), BF16),
        ((blocks * LANES, LANES), BF16),
        ((leaves // NODES, LANES, NODES * leaf_points), BF16),
        ((vectors, (2 * leaves // NODES - 1) * LANES), F32),
        ((RANK, LANES), F32),
        ((3 * leaves, RANK * vectors), F32),
        ((members * RANK, LANES), F32),
        ((groups * RANK, LANES), F32),
        ((2 * RANK, members * RANK), BF16),
        ((2, 3 * RANK, (members + groups) * RANK), BF16),
        ((vectors, leaves * RANK), F32),
        ((leaves * RANK, 2 * pairs * RANK // 2), BF16),
        ((leaves * RANK, 2 * pairs * RANK // 2), BF16),
        ((vectors, 3 * RANK), F32),
    ]
    whole = pl.BlockSpec(memory_space=pltpu.VMEM)
    kept = pl.pallas_call(
        functools.partial(kernel, (n_lat, groups, members)),
        out_shape=(
            jax.ShapeDtypeStruct((vectors, points), F32),
            jax.ShapeDtypeStruct((3 * RANK, points), BF16),
            jax.ShapeDtypeStruct((vectors, 3 * RANK), BF16),
        ),
        in_specs=[pl.BlockSpec(memory_space=pltpu.HBM)] * len(operands),
        out_specs=(whole, whole, whole),
        scratch_shapes=[pltpu.VMEM(shape, dtype) for shape, dtype in scratch]
        + [
            pltpu.SemaphoreType.DMA((len(operands),)),
            pltpu.SemaphoreType.DMA((members,)),
            pltpu.SemaphoreType.DMA((groups,)),
            pltpu.SemaphoreType.DMA((groups,)),
            pltpu.SemaphoreType.DMA((4,)),
            pltpu.SemaphoreType.DMA((members,)),
            pltpu.SemaphoreType.DMA((groups,)),
            pltpu.SemaphoreType.DMA((4,)),
            pltpu.SemaphoreType.REGULAR((members,)),
            pltpu.SemaphoreType.REGULAR((groups,)),
            pltpu.SemaphoreType.REGULAR((4,)),
        ],
        compiler_params=pltpu.CompilerParams(
            collective_id=0, has_side_effects=True, vmem_limit_bytes=40 * 2**20
        ),
        name="h2_tree",
    )(*[pltpu.with_memory_space_constraint(operand, pltpu.HBM) for operand in operands])
    return pl.pallas_call(
        last_part,
        out_shape=jax.ShapeDtypeStruct((vectors, points), F32),
        in_specs=[whole] * 3,
        out_specs=pl.BlockSpec(memory_space=pltpu.HBM),
        scratch_shapes=[pltpu.VMEM((vectors, points), F32), pltpu.SemaphoreType.DMA((4,))],
        compiler_params=pltpu.CompilerParams(vmem_limit_bytes=8 * 2**20),
        name="h2_last",
    )(*kept)


def solution(mesh):
    return jax.shard_map(
        functools.partial(shards, mesh.shape["lat"], mesh.shape["lon"]),
        mesh=mesh,
        in_specs=(
            P(None, ("lat", "lon")),
            P(None, ("lat", "lon")),
            P(("lat", "lon"), None, None),
            P(("lat", "lon"), None, None, None),
            P(("lat", "lon"), None, None, None),
            P("lat", None, None, None),
            P("lat", None, None, None),
            P("lat", "lon", None),
            P("lat", "lon", None),
            P("lat", "lon", None, None, None),
        ),
        out_specs=P(None, ("lat", "lon")),
        check_vma=False,
    )
```

time: 30.3 us -> 27.6 us (0.911)
  the two profiles are of different devices: /device:TPU:1 before, /device:TPU:480 now
where the time goes in v3:
time: 27.6 us; the launch traced here: 27.5 us
  Pallas kernels  27.5 us (100%)
    pallas_call x1, Pallas kernels, shards(): pl.pallas_call(functools.partial(kernel, (n_lat, groups, members)), out_s...  26.5 us
    pallas_call x1, Pallas kernels, shards(): pl.pallas_call(last_part, out_shape=jax.ShapeDtypeStruct((vectors, points...  0.96 us

profile of v3, /device:TPU:480, one launch (start us, length us, event | category | flops | bytes accessed | tf_op | source)
XLA Modules:
  0.0 27.5 jit_solution(16263864873150878256)
XLA Ops:
  0.0 26.5 %h2_tree.1 = (f32[64,2048]{1,0:T(8,128)S(1)}, bf16[48,2048]{1,0:T(8,128)(2,1)S(1)}, bf16[64,48]{1,0:T(8,128)(2,1)S(1)}) custom-call(bf16[64,2048]{1,0:T(8,128)(2,1)} %ensemble.1, bf16[16,2048]{1,0:T(8,128)(2,1)} %basis.1, bf16[32,64,320]{2,1,0:T(8,128)(2,1)} %near.1, f32[256,64]{1,0:T(8,128)} %bitcast.29, f32[256,64]{1,0:T(8,128)} %bitcast.30, ...), custom_call_target="tpu_custom_call" | custom-call | tf_op jit(solution)/shard_map/h2_tree/pallas_call | solution.py:750
  26.5 1.0 %h2_last.1 = f32[64,2048]{1,0:T(8,128)} custom-call(f32[64,2048]{1,0:T(8,128)S(1)} %get-tuple-element.8.acc_ref, bf16[48,2048]{1,0:T(8,128)(2,1)S(1)} %get-tuple-element.9.final_ref, bf16[64,48]{1,0:T(8,128)(2,1)S(1)} %get-tuple-element.10.down_ref), custom_call_target="tpu_custom_call" | custom-call | tf_op jit(solution)/shard_map/h2_last/pallas_call | solution.py:778

commit v4 on v3

--- a/solution.py
+++ b/solution.py
@@ -11,6 +11,7 @@
 BF16 = jnp.bfloat16
 RANK = 16
 LANES = 128
+HALF = RANK // 2
 NODES = 8
 MESH = pl.DeviceIdType.MESH
 
@@ -60,12 +61,13 @@
     return tuple(ref[pl.ds(first * LANES, count * LANES), :] for ref in refs)
 
 
-def each(low, high, act):
-    def step(index, carry):
-        act(index)
-        return carry
-
-    lax.fori_loop(low, high, step, 0)
+def each(count, wanted, act):
+    for turn in range(count):
+        pl.when(wanted(turn))(functools.partial(act, turn))
+
+
+def wait(semaphore, count):
+    pl.when(count > 0)(lambda: pl.semaphore_wait(semaphore, count))
 
 
 def turn_of(index, count):
@@ -144,13 +146,12 @@
     return level
 
 
-def stacked(blocks):
-    count = blocks
+def stacked(count, half):
     members = min(count, NODES)
     offset = count if count < NODES else 0
-    row = iota((members * RANK, LANES), 0)
-    lane = iota((members * RANK, LANES), 1)
-    return one_hot(lane == (row % RANK) * NODES + row // RANK + offset)
+    row = iota((members * HALF, LANES), 0)
+    lane = iota((members * HALF, LANES), 1)
+    return one_hot(lane == (half * HALF + row % HALF) * NODES + row // HALF + offset)
 
 
 def operators(turned, masks, edge_refs, block, spread):
@@ -195,12 +196,9 @@
     basis_ref,
     near_ref,
     le_ref,
-    ll_ref,
-    ue_ref,
-    ul_ref,
-    src_ref,
-    tgt_ref,
-    pl_ref,
+    linked_ref,
+    upper_ref,
+    pairs_ref,
     eh_ref,
     el_ref,
     vh_ref,
@@ -228,6 +226,7 @@
     member_in,
     group_in,
     side_in,
+    last_in,
 ):
     n_lat, groups, members = sizes
     n_lon = groups * members
@@ -272,33 +271,31 @@
     mirror = [1, 0, 3, 2]
 
     own_points = x_ref.at[:, halo : halo + points]
-    loads = [
-        pltpu.make_async_copy(src, dst, load_sem.at[i])
-        for i, (src, dst) in enumerate(
-            [
-                (local_edge, le_ref),
-                (basis, basis_ref),
-                (ensemble, own_points),
-                (local_link, ll_ref),
-                (upper_edge, ue_ref),
-                (upper_link, ul_ref),
-                (source, src_ref),
-                (target, tgt_ref),
-                (pair_link, pl_ref),
-                (near, near_ref),
-            ]
-        )
+    sources = [
+        (0, local_edge, le_ref),
+        (1, basis, basis_ref),
+        (2, ensemble, own_points),
+        (3, upper_edge, upper_ref.at[0]),
+        (3, upper_link, upper_ref.at[1]),
+        (4, local_link, linked_ref.at[0]),
+        (4, pair_link, linked_ref.at[1]),
+        (5, source, pairs_ref.at[0]),
+        (5, target, pairs_ref.at[1]),
+        (6, near, near_ref),
     ]
-    for load in loads:
-        load.start()
+    for i, src, dst in sources:
+        pltpu.make_async_copy(src, dst, load_sem.at[i]).start()
+
+    def loaded(i, ref):
+        pltpu.make_async_copy(ref, ref, load_sem.at[i]).wait()
 
     barrier = pltpu.get_barrier_semaphore()
 
     def signal(semaphore, peer):
         pl.semaphore_signal(semaphore, inc=1, device_id=peer, device_id_type=MESH)
 
-    each(member_turn + 1, members, lambda t: signal(barrier, member_at(member_by(t))))
-    each(group_turn + 1, groups, lambda t: signal(barrier, group_at(group_by(t))))
+    each(members, lambda t: t > member_turn, lambda t: signal(barrier, member_at(member_by(t))))
+    each(groups, lambda t: t > group_turn, lambda t: signal(barrier, group_at(group_by(t))))
     for there, peer in zip(later, beside_at):
         pl.when(there)(functools.partial(signal, barrier, peer))
     stand_in = flat == 1
@@ -308,11 +305,22 @@
     heard = member_turn + group_turn + jnp.where(stand_in, groups - 1, 0)
     for there in earlier:
         heard = heard + jnp.where(there, 1, 0)
-    pl.semaphore_wait(barrier, heard)
-    each(0, member_turn, lambda t: signal(member_in.at[member], member_at(member_by(t))))
-    each(0, group_turn, lambda t: signal(group_in.at[group], group_at(group_by(t))))
-    for k in range(4):
-        pl.when(earlier[k])(functools.partial(signal, side_in.at[mirror[k]], beside_at[k]))
+    wait(barrier, heard)
+    is_last = flat == 0
+
+    @pl.when(is_last)
+    def _():
+        for j in range(1, members):
+            signal(last_in, member_at(j))
+        pl.when(above)(lambda: signal(last_in, above_at))
+
+    @pl.when(flat > 0)
+    def _():
+        each(members, lambda t: t < member_turn, lambda t: signal(member_in, member_at(member_by(t))))
+        for k in range(4):
+            pl.when(earlier[k])(functools.partial(signal, side_in, beside_at[k]))
+
+    each(groups, lambda t: t < group_turn, lambda t: signal(group_in, group_at(group_by(t))))
 
     row, lane = iota((LANES, LANES), 0), iota((LANES, LANES), 1)
     offset = row - lane // NODES
@@ -350,8 +358,9 @@
     group_base = local_blocks + member_blocks
     group_e, group_v = reader(edges, group_base), reader(links, group_base)
 
-    for load in loads[:3]:
-        load.wait()
+    loaded(0, le_ref)
+    loaded(1, basis_ref)
+    loaded(2, own_points)
     operators(turned(le_ref, eye), local_masks[0], edges, 0, spread)
     width = NODES * leaf_points
     leaf_blocks = leaves // NODES
@@ -378,9 +387,8 @@
     top_ref[...] = top
     for i, block in enumerate([eighth] + halves + across):
         ups_ref[:, i * LANES : (i + 1) * LANES] = block
-    empty = jnp.zeros((RANK, LANES - vectors), F32)
-    own_member = members_ref.at[pl.ds(member * RANK, RANK)]
-    own_member[...] = side_by_side([device_sum, empty])
+    own_member = members_ref.at[pl.ds(member * HALF, HALF)]
+    own_member[...] = side_by_side([device_sum[:HALF], device_sum[HALF:]])
 
     def copy_to(src, dst, sent, arrived, peer):
         return pltpu.make_async_remote_copy(
@@ -393,23 +401,23 @@
         )
 
     def member_copy(j):
-        return copy_to(own_member, own_member, member_send.at[j], member_sem.at[member], member_at(j))
-
-    def member_arrival(j):
-        there = members_ref.at[pl.ds(j * RANK, RANK)]
-        return copy_to(there, there, member_send.at[j], member_sem.at[j], member_at(j))
-
-    own_group = groups_ref.at[pl.ds(group * RANK, RANK)]
+        return copy_to(own_member, own_member, member_send, member_sem, member_at(j))
+
+    own_group = groups_ref.at[pl.ds(group * HALF, HALF)]
 
     def group_copy(j):
-        return copy_to(own_group, own_group, group_send.at[j], group_sem.at[group], group_at(j))
+        return copy_to(own_group, own_group, group_send, group_sem, group_at(j))
 
     def stand_in_copy(j):
-        return copy_to(own_group, own_group, stand_in_send.at[j], group_sem.at[0], (lat, j * members))
-
-    def group_arrival(j):
-        there = groups_ref.at[pl.ds(j * RANK, RANK)]
-        return copy_to(there, there, group_send.at[j], group_sem.at[j], group_at(j))
+        return copy_to(own_group, own_group, stand_in_send, group_sem, (lat, j * members))
+
+    def all_members():
+        part = members_ref.at[0 : (members - 1) * HALF]
+        return copy_to(part, part, member_send, member_sem, member_at(member_by(0)))
+
+    def all_groups(sent):
+        part = groups_ref.at[0 : (groups - 1) * HALF]
+        return copy_to(part, part, sent, group_sem, group_at(group_by(0)))
 
     own_sums = ext_ref.at[leaves : 2 * leaves]
     first_halo, last_halo = x_ref.at[:, halo : 2 * halo], x_ref.at[:, points : points + halo]
@@ -422,19 +430,7 @@
     from_before, from_after, from_below, from_above = to_after, to_before, to_above, to_below
     side_copies = [to_after, to_before, to_above, to_below]
 
-    def to_member(j):
-        pl.semaphore_wait(member_in.at[j], 1)
-        member_copy(j).start()
-
-    def to_group(j):
-        pl.semaphore_wait(group_in.at[j], 1)
-        group_copy(j).start()
-
-    def to_side(k):
-        pl.semaphore_wait(side_in.at[k], 1)
-        side_copies[k].start()
-
-    each(0, member_turn, lambda t: member_copy(member_by(member_turn - 1 - t)).start())
+    each(members, lambda t: t < member_turn, lambda t: member_copy(member_by(t)).start())
     for k in range(2):
         pl.when(earlier[k])(side_copies[k].start)
 
@@ -462,17 +458,15 @@
     wanted = jnp.where(slot < member_slots, slot + (groups + group - 1) * scale, slot - member_slots)
     chosen = one_hot(wanted == iota((upper_rows, upper_nodes), 1))
     upper_masks = masks(upper_rows, lambda r: jnp.where(r < member_slots, r, r - member_slots))
-    loads[4].wait()
-    operators(turned(ue_ref, chosen), upper_masks[0], edges, local_blocks, spread)
-
-    per_block = min(members, NODES) * RANK
-    member_order = stacked(members)
-    member_paths = paths(members, member_e)
-    for i, block in enumerate(member_paths):
-        cut = slice(i * per_block, (i + 1) * per_block)
-        high, low = split(picked_by(nt, split(block), member_order))
-        to_group_ref[0:RANK, cut] = high
-        to_group_ref[RANK : 2 * RANK, cut] = low
+    loaded(3, upper_ref)
+    operators(turned(upper_ref.at[0], chosen), upper_masks[0], edges, local_blocks, spread)
+
+    member_order = [stacked(members, half) for half in range(2)]
+    member_paths = [split(block) for block in paths(members, member_e)]
+    for half in range(2):
+        parts = [picked_by(nt, block, member_order[half]) for block in member_paths]
+        for i, part in enumerate(split(side_by_side(parts) if len(parts) > 1 else parts[0])):
+            to_group_ref[i, half * RANK : (half + 1) * RANK, :] = part
 
     blank = jnp.zeros((leaf_points, leaf_points), BF16)
     pair_points = 2 * leaf_points
@@ -489,11 +483,10 @@
         part = nt(window, weights)
         acc_ref[:, cut] = acc_ref[:, cut] + part if add else part
 
-    def local_work():
-        for load in loads[3:4] + loads[5:]:
-            load.wait()
-        operators(turned(ul_ref, chosen), upper_masks[1], links, local_blocks, spread)
-        operators(turned(ll_ref, eye), local_masks[1], links, 0, spread)
+    def maps_work():
+        loaded(4, linked_ref)
+        operators(turned(upper_ref.at[1], chosen), upper_masks[1], links, local_blocks, spread)
+        operators(turned(linked_ref.at[0], eye), local_masks[1], links, 0, spread)
 
         own_rows, own_lanes = iota((RANK, LANES), 0), iota((RANK, LANES), 1)
         starts = []
@@ -506,14 +499,18 @@
         place = one_hot((row // NODES == lane // NODES) & (row % NODES == 1) & (lane % NODES == group_slot))
         placed = picked_by(nn, split(three(nn, split(member_ups[0]), member_e(0, 1))), place)
         group_ups = climb([placed], groups, group_e)
-        maps = [
-            picked_by(nt, split(block), member_order)
-            for block in descend(member_ups, members, member_e, member_v, nn)
+        trees = [
+            (descend(member_ups, members, member_e, member_v, nn), members),
+            (descend(group_ups, groups, group_e, group_v, nn), groups),
         ]
-        maps.append(picked_by(nt, split(descend(group_ups, groups, group_e, group_v, nn)[0]), stacked(groups)))
+        maps = []
+        for blocks, count in trees:
+            parts = [split(block) for block in blocks]
+            maps += [picked_by(nt, part, stacked(count, half)) for half in range(2) for part in parts]
         for i, part in enumerate(split(side_by_side(maps))):
             map_ref[i] = jnp.concatenate([part] * 3, axis=0)
 
+    def local_work():
         local_ups = {i + 1: ups_ref[:, i * LANES : (i + 1) * LANES] for i in range(2 * leaf_blocks - 1)}
         for j, block in enumerate(descend(crown(local_ups, local_e), leaves, local_e, local_v, nt)):
             local_down_ref[:, j * LANES : (j + 1) * LANES] = block
@@ -524,13 +521,15 @@
             final_ref[RANK : 2 * RANK, cut] = folded[0]
             final_ref[2 * RANK : 3 * RANK, cut] = folded[1]
 
+        loaded(6, near_ref)
         for j in range(leaves // 2):
             low, high = (halo if j == 0 else 0), (span - halo if j == leaves // 2 - 1 else span)
             near_part(j, low, high, False)
 
-        wide_target = side_by_side([tgt_ref[...], tgt_ref[...]])
+        loaded(5, pairs_ref)
+        wide_target = side_by_side([pairs_ref[1], pairs_ref[1]])
         hits = jnp.where(iota((leaves, 2 * pairs), 0) == wide_target, 1.0, 0.0)
-        link_rows = pl_ref[...].reshape(RANK, 2, half, pairs)
+        link_rows = linked_ref[1].reshape(RANK, 2, half, pairs)
         link_rows = jnp.concatenate([link_rows[:, 0], link_rows[:, 1]], axis=2)
         link_high = link_rows.astype(BF16).astype(F32)
         for ref, part in ((pair_high_ref, link_high), (pair_low_ref, link_rows - link_high)):
@@ -541,15 +540,28 @@
                         [hit * part[a, k : k + 1] for a in range(RANK)], axis=0
                     ).astype(BF16)
 
+    wait(side_in, jnp.where(later[0], 1, 0) + jnp.where(later[2], 1, 0))
     for k in (0, 2):
-        pl.when(later[k])(functools.partial(to_side, k))
+        pl.when(later[k])(side_copies[k].start)
 
     def late_sends():
-        each(member_turn + 1, members - member_shift, lambda t: to_member(member_by(t)))
+        last = members - member_shift
+        wait(member_in, last - 1 - member_turn)
+        each(members, lambda t: (t > member_turn) & (t < last), lambda t: member_copy(member_by(t)).start())
 
     def beside():
+        by_last = (member_shift == 1) & (flat > 0)
+
+        @pl.when(by_last | later[3])
+        def _():
+            pl.semaphore_wait(last_in, 1)
+
+        @pl.when(by_last)
+        def _():
+            member_copy(0).start()
+
         for k in (1, 3):
-            pl.when(later[k])(functools.partial(to_side, k))
+            pl.when(later[k])(side_copies[k].start)
 
         pl.when(below)(from_below.wait_recv)
         pl.when(above)(from_above.wait_recv)
@@ -563,7 +575,7 @@
             above_sums[...] = jnp.zeros(above_sums.shape, F32)
 
         spot = iota((3 * leaves, pairs), 0)
-        reads = jnp.where(spot == src_ref[...], 1.0, 0.0)
+        reads = jnp.where(spot == pairs_ref[0], 1.0, 0.0)
         reads = jnp.transpose(reads).astype(BF16)
         found = [nn(reads, part) for part in split(ext_ref[...])]
         left_side = iota((pairs, LANES), 1) < vectors
@@ -596,29 +608,29 @@
         near_part(leaves // 2 - 1, span - halo, span, True)
 
     def relay():
-        @pl.when((member_shift == 1) & (member_turn < members - 1))
-        def _():
-            to_member(0)
-
-        each(0, member, lambda j: member_arrival(j).wait_recv())
-        each(member + 1, members, lambda j: member_arrival(j).wait_recv())
-        own_group[...] = three(
-            nn, (to_group_ref[0:RANK, :], to_group_ref[RANK : 2 * RANK, :]), split(members_ref[...])
-        )
+        all_members().wait_recv()
+        both = three(nn, (to_group_ref[0], to_group_ref[1]), split(members_ref[...]))
+        group_sum = both[:RANK, :vectors] + both[RANK:, vectors:]
+        own_group[...] = side_by_side([group_sum[:HALF], group_sum[HALF:]])
+
         @pl.when(flat > 0)
         def _():
-            each(0, group_turn, lambda t: group_copy(group_by(group_turn - 1 - t)).start())
+            each(groups, lambda t: t < group_turn, lambda t: group_copy(group_by(t)).start())
+
+        wait(group_in, groups - 1 - group_turn)
+        each(groups, lambda t: t > group_turn, lambda t: group_copy(group_by(t)).start())
 
         @pl.when(stand_in)
         def _():
-            each(1, groups, lambda j: stand_in_copy(j).start())
-
-        each(group_turn + 1, groups, lambda t: to_group(group_by(t)))
+            for j in range(1, groups):
+                stand_in_copy(j).start()
+
+    maps_work()
+    late_sends()
 
     def stage(step, carry):
-        turn = jnp.where((lat == 0) | (step == 0), step, 3 - step)
+        turn = jnp.where((member_shift == 1) | (step == 0), step, 3 - step)
         pl.when(turn == 0)(local_work)
-        pl.when(step == 0)(late_sends)
         pl.when(turn == 1)(beside)
         pl.when(turn == 2)(relay)
         return carry
@@ -626,13 +638,13 @@
     lax.fori_loop(0, 3, stage, 0)
 
     def mapped(ref, first, count):
+        turned_sums = jnp.transpose(ref[...])
+        turned_sums = split(side_by_side([turned_sums[:vectors], turned_sums[vectors:]]))
         cut = slice(first * RANK, (first + count) * RANK)
-        turned_sums = jnp.transpose(ref[...])[:vectors]
-        return three(nt, split(turned_sums), (map_ref[0][:, cut], map_ref[1][:, cut]))
+        return three(nt, turned_sums, (map_ref[0][:, cut], map_ref[1][:, cut]))
 
     here_ref[...] = mapped(members_ref, 0, members)
-    each(0, group, lambda j: group_arrival(j).wait_recv())
-    each(group + 1, groups, lambda j: group_arrival(j).wait_recv())
+    all_groups(group_send).wait_recv()
     down_here = here_ref[...] + mapped(groups_ref, members, groups)
     down_parts = split(down_here)
     lanes3 = iota(down_here.shape, 1)
@@ -640,37 +652,24 @@
     down3 = jnp.where(middle, down_parts[1].astype(F32), down_parts[0].astype(F32))
     down_ref[...] = down3.astype(BF16)
 
-    each(0, member, lambda j: member_copy(j).wait_send())
-    each(member + 1, members, lambda j: member_copy(j).wait_send())
-
-    @pl.when(flat > 0)
-    def _():
-        each(0, group, lambda j: group_copy(j).wait_send())
-        each(group + 1, groups, lambda j: group_copy(j).wait_send())
-
-    @pl.when(stand_in)
-    def _():
-        each(1, groups, lambda j: stand_in_copy(j).wait_send())
-
+    all_members().wait_send()
+    pl.when(flat > 0)(all_groups(group_send).wait_send)
+    pl.when(stand_in)(all_groups(stand_in_send).wait_send)
     pl.when(after)(to_after.wait_send)
     pl.when(before)(to_before.wait_send)
     pl.when(above)(to_above.wait_send)
     pl.when(below)(to_below.wait_send)
 
 
-def last_part(acc_ref, final_ref, down_ref, out_ref, held_ref, sems):
+def last_part(acc_ref, final_ref, down_ref, out_ref, held_ref, sem):
     down3 = down_ref[...]
     points = out_ref.shape[1]
     width = points // 4
-    copies = []
     for j in range(4):
         cut = slice(j * width, (j + 1) * width)
         held_ref[:, cut] = acc_ref[:, cut] + nn(down3, final_ref[:, cut])
-        copy = pltpu.make_async_copy(held_ref.at[:, cut], out_ref.at[:, cut], sems.at[j])
-        copy.start()
-        copies.append(copy)
-    for copy in copies:
-        copy.wait()
+        pltpu.make_async_copy(held_ref.at[:, cut], out_ref.at[:, cut], sem).start()
+    pltpu.make_async_copy(held_ref, out_ref, sem).wait()
 
 
 def split_lon(n_lon):
@@ -723,12 +722,9 @@
         ((RANK, points), BF16),
         (near_blocks.shape, BF16),
         ((RANK * RANK, 2 * leaves), F32),
-        ((RANK * RANK, 2 * leaves), F32),
-        ((RANK * RANK, upper_nodes), F32),
-        ((RANK * RANK, upper_nodes), F32),
-        ((1, pairs), jnp.int32),
-        ((1, pairs), jnp.int32),
-        ((RANK * RANK, pairs), F32),
+        ((2, RANK * RANK, 2 * leaves), F32),
+        ((2, RANK * RANK, upper_nodes), F32),
+        ((2, 1, pairs), jnp.int32),
         ((blocks * LANES, LANES), BF16),
         ((blocks * LANES, LANES), BF16),
         ((blocks * LANES, LANES), BF16),
@@ -737,9 +733,9 @@
         ((vectors, (2 * leaves // NODES - 1) * LANES), F32),
         ((RANK, LANES), F32),
         ((3 * leaves, RANK * vectors), F32),
-        ((members * RANK, LANES), F32),
-        ((groups * RANK, LANES), F32),
-        ((2 * RANK, members * RANK), BF16),
+        ((members * HALF, LANES), F32),
+        ((groups * HALF, LANES), F32),
+        ((2, 2 * RANK, members * HALF), BF16),
         ((2, 3 * RANK, (members + groups) * RANK), BF16),
         ((vectors, leaves * RANK), F32),
         ((leaves * RANK, 2 * pairs * RANK // 2), BF16),
@@ -758,17 +754,18 @@
         out_specs=(whole, whole, whole),
         scratch_shapes=[pltpu.VMEM(shape, dtype) for shape, dtype in scratch]
         + [
-            pltpu.SemaphoreType.DMA((len(operands),)),
-            pltpu.SemaphoreType.DMA((members,)),
-            pltpu.SemaphoreType.DMA((groups,)),
-            pltpu.SemaphoreType.DMA((groups,)),
+            pltpu.SemaphoreType.DMA((7,)),
+            pltpu.SemaphoreType.DMA,
+            pltpu.SemaphoreType.DMA,
+            pltpu.SemaphoreType.DMA,
             pltpu.SemaphoreType.DMA((4,)),
-            pltpu.SemaphoreType.DMA((members,)),
-            pltpu.SemaphoreType.DMA((groups,)),
+            pltpu.SemaphoreType.DMA,
+            pltpu.SemaphoreType.DMA,
             pltpu.SemaphoreType.DMA((4,)),
-            pltpu.SemaphoreType.REGULAR((members,)),
-            pltpu.SemaphoreType.REGULAR((groups,)),
-            pltpu.SemaphoreType.REGULAR((4,)),
+            pltpu.SemaphoreType.REGULAR,
+            pltpu.SemaphoreType.REGULAR,
+            pltpu.SemaphoreType.REGULAR,
+            pltpu.SemaphoreType.REGULAR,
         ],
         compiler_params=pltpu.CompilerParams(
             collective_id=0, has_side_effects=True, vmem_limit_bytes=40 * 2**20
@@ -780,7 +777,7 @@
         out_shape=jax.ShapeDtypeStruct((vectors, points), F32),
         in_specs=[whole] * 3,
         out_specs=pl.BlockSpec(memory_space=pltpu.HBM),
-        scratch_shapes=[pltpu.VMEM((vectors, points), F32), pltpu.SemaphoreType.DMA((4,))],
+        scratch_shapes=[pltpu.VMEM((vectors, points), F32), pltpu.SemaphoreType.DMA],
         compiler_params=pltpu.CompilerParams(vmem_limit_bytes=8 * 2**20),
         name="h2_last",
     )(*kept)

time: 27.6 us -> 24 us (0.87)
  the two profiles are of different devices: /device:TPU:480 before, /device:TPU:384 now
where the time goes in v4:
time: 24 us; the launch traced here: 23.9 us
  Pallas kernels  23.9 us (100%)
    pallas_call x1, Pallas kernels, shards(): pl.pallas_call(functools.partial(kernel, (n_lat, groups, members)), out_s...  22.9 us
    pallas_call x1, Pallas kernels, shards(): pl.pallas_call(last_part, out_shape=jax.ShapeDtypeStruct((vectors, points...  0.93 us

profile of v4, /device:TPU:384, one launch (start us, length us, event | category | flops | bytes accessed | tf_op | source)
XLA Modules:
  0.0 23.9 jit_solution(11383973485446430878)
XLA Ops:
  0.0 22.9 %h2_tree.1 = (f32[64,2048]{1,0:T(8,128)S(1)}, bf16[48,2048]{1,0:T(8,128)(2,1)S(1)}, bf16[64,48]{1,0:T(8,128)(2,1)S(1)}) custom-call(bf16[64,2048]{1,0:T(8,128)(2,1)} %ensemble.1, bf16[16,2048]{1,0:T(8,128)(2,1)} %basis.1, bf16[32,64,320]{2,1,0:T(8,128)(2,1)} %near.1, f32[256,64]{1,0:T(8,128)} %bitcast.29, f32[256,64]{1,0:T(8,128)} %bitcast.30, ...), custom_call_target="tpu_custom_call" | custom-call | tf_op jit(solution)/shard_map/h2_tree/pallas_call | solution.py:746
  22.9 0.9 %h2_last.1 = f32[64,2048]{1,0:T(8,128)} custom-call(f32[64,2048]{1,0:T(8,128)S(1)} %get-tuple-element.8.acc_ref, bf16[48,2048]{1,0:T(8,128)(2,1)S(1)} %get-tuple-element.9.final_ref, bf16[64,48]{1,0:T(8,128)(2,1)S(1)} %get-tuple-element.10.down_ref), custom_call_target="tpu_custom_call" | custom-call | tf_op jit(solution)/shard_map/h2_last/pallas_call | solution.py:775

commit v5 on v4

--- a/solution.py
+++ b/solution.py
@@ -283,8 +283,11 @@
         (5, target, pairs_ref.at[1]),
         (6, near, near_ref),
     ]
-    for i, src, dst in sources:
-        pltpu.make_async_copy(src, dst, load_sem.at[i]).start()
+    def load(some):
+        for i, src, dst in some:
+            pltpu.make_async_copy(src, dst, load_sem.at[i]).start()
+
+    load(sources[:3])
 
     def loaded(i, ref):
         pltpu.make_async_copy(ref, ref, load_sem.at[i]).wait()
@@ -321,6 +324,8 @@
             pl.when(earlier[k])(functools.partial(signal, side_in, beside_at[k]))
 
     each(groups, lambda t: t < group_turn, lambda t: signal(group_in, group_at(group_by(t))))
+
+    load(sources[3:])
 
     row, lane = iota((LANES, LANES), 0), iota((LANES, LANES), 1)
     offset = row - lane // NODES
@@ -629,7 +634,9 @@
     late_sends()
 
     def stage(step, carry):
-        turn = jnp.where((member_shift == 1) | (step == 0), step, 3 - step)
+        turn = jnp.where(
+            member_shift == 1, step, jnp.where(member < cores, lax.rem(step + 2, 3), jnp.where(step == 0, 0, 3 - step))
+        )
         pl.when(turn == 0)(local_work)
         pl.when(turn == 1)(beside)
         pl.when(turn == 2)(relay)

time: 24 us -> 23.7 us (0.987)
  the two profiles are of different devices: /device:TPU:384 before, /device:TPU:416 now
where the time goes in v5:
time: 23.7 us; the launch traced here: 23.5 us
  Pallas kernels  23.5 us (99%)
    pallas_call x1, Pallas kernels, shards(): pl.pallas_call(functools.partial(kernel, (n_lat, groups, members)), out_s...  22.6 us
    pallas_call x1, Pallas kernels, shards(): pl.pallas_call(last_part, out_shape=jax.ShapeDtypeStruct((vectors, points...  0.94 us

profile of v5, /device:TPU:416, one launch (start us, length us, event | category | flops | bytes accessed | tf_op | source)
XLA Modules:
  0.0 23.5 jit_solution(1189318900576035968)
XLA Ops:
  0.0 22.6 %h2_tree.1 = (f32[64,2048]{1,0:T(8,128)S(1)}, bf16[48,2048]{1,0:T(8,128)(2,1)S(1)}, bf16[64,48]{1,0:T(8,128)(2,1)S(1)}) custom-call(bf16[64,2048]{1,0:T(8,128)(2,1)} %ensemble.1, bf16[16,2048]{1,0:T(8,128)(2,1)} %basis.1, bf16[32,64,320]{2,1,0:T(8,128)(2,1)} %near.1, f32[256,64]{1,0:T(8,128)} %bitcast.29, f32[256,64]{1,0:T(8,128)} %bitcast.30, ...), custom_call_target="tpu_custom_call" | custom-call | tf_op jit(solution)/shard_map/h2_tree/pallas_call | solution.py:753
  22.6 0.9 %h2_last.1 = f32[64,2048]{1,0:T(8,128)} custom-call(f32[64,2048]{1,0:T(8,128)S(1)} %get-tuple-element.8.acc_ref, bf16[48,2048]{1,0:T(8,128)(2,1)S(1)} %get-tuple-element.9.final_ref, bf16[64,48]{1,0:T(8,128)(2,1)S(1)} %get-tuple-element.10.down_ref), custom_call_target="tpu_custom_call" | custom-call | tf_op jit(solution)/shard_map/h2_last/pallas_call | solution.py:782

commit v6 on v5

--- a/solution.py
+++ b/solution.py
@@ -671,8 +671,8 @@
 def last_part(acc_ref, final_ref, down_ref, out_ref, held_ref, sem):
     down3 = down_ref[...]
     points = out_ref.shape[1]
-    width = points // 4
-    for j in range(4):
+    width = points // 8
+    for j in range(8):
         cut = slice(j * width, (j + 1) * width)
         held_ref[:, cut] = acc_ref[:, cut] + nn(down3, final_ref[:, cut])
         pltpu.make_async_copy(held_ref.at[:, cut], out_ref.at[:, cut], sem).start()

time: 23.7 us -> 23.7 us (level)
  no operation moved by 1% of the time
where the time goes in v6:
time: 23.7 us; the launch traced here: 23.5 us
  Pallas kernels  23.5 us (99%)
    pallas_call x1, Pallas kernels, shards(): pl.pallas_call(functools.partial(kernel, (n_lat, groups, members)), out_s...  22.6 us
    pallas_call x1, Pallas kernels, shards(): pl.pallas_call(last_part, out_shape=jax.ShapeDtypeStruct((vectors, points...  0.93 us

profile of v6, /device:TPU:416, one launch (start us, length us, event | category | flops | bytes accessed | tf_op | source)
XLA Modules:
  0.0 23.5 jit_solution(9798761112871611770)
XLA Ops:
  0.0 22.6 %h2_tree.1 = (f32[64,2048]{1,0:T(8,128)S(1)}, bf16[48,2048]{1,0:T(8,128)(2,1)S(1)}, bf16[64,48]{1,0:T(8,128)(2,1)S(1)}) custom-call(bf16[64,2048]{1,0:T(8,128)(2,1)} %ensemble.1, bf16[16,2048]{1,0:T(8,128)(2,1)} %basis.1, bf16[32,64,320]{2,1,0:T(8,128)(2,1)} %near.1, f32[256,64]{1,0:T(8,128)} %bitcast.29, f32[256,64]{1,0:T(8,128)} %bitcast.30, ...), custom_call_target="tpu_custom_call" | custom-call | tf_op jit(solution)/shard_map/h2_tree/pallas_call | solution.py:753
  22.6 0.9 %h2_last.1 = f32[64,2048]{1,0:T(8,128)} custom-call(f32[64,2048]{1,0:T(8,128)S(1)} %get-tuple-element.8.acc_ref, bf16[48,2048]{1,0:T(8,128)(2,1)S(1)} %get-tuple-element.9.final_ref, bf16[64,48]{1,0:T(8,128)(2,1)S(1)} %get-tuple-element.10.down_ref), custom_call_target="tpu_custom_call" | custom-call | tf_op jit(solution)/shard_map/h2_last/pallas_call | solution.py:782
